TPU v7x, 32 devices: a whole 2x2x4 slice. The times are simulated.
32 devices in a mesh: group: 2 (over y), weight: 4 (over z), dp: 4 (over x, core).
Axes of the slice: x: 2, y: 2, z: 4, core: 2. Of those that a mesh axis runs over, the one named last changes fastest.
Arguments:
- tapped: bfloat16 [3, 4096, 4096], P(None, ('group', 'dp'), 'weight'), parts along dimension 1, may hold values from -6 to 6
- join_weight: bfloat16 [3, 4096, 4096], P(None, 'weight', 'dp')
- norm_gain: float32 [4096], P('weight'), may hold values from 0.1 to 1.9
- cotangent: bfloat16 [4096, 4096], P(('group', 'dp'), 'weight'), parts along dimension 0, may hold values from -0.13183594 to 0.13183594
- live_mask: int32 [4096], P(('group', 'dp')), parts along dimension 0, may hold values 0 or 1
Outputs:
- hidden: bfloat16 [4096, 4096], P(('group', 'dp'), 'weight'), parts along dimension 0
- grad_weight: bfloat16 [6, 4096, 4096], P('group', 'weight'), parts along dimension 0
- grad_gain: float32 [8192], P(('group', 'weight')), parts along dimension 0
There are 2 independent parts, one for each index of `group`. A program takes and returns all parts, laid end to end along the dimension named above; an argument that names none is the same for every part. Nothing has to cross between parts.
All inputs are finite; a program needn't handle non-finite values. No bound on the sum of `live_mask` on one device may be relied on, other than what follows from the above.
Results may differ from a plain program's by a relative error of at most 0.014.
Values may be sent and summed in bfloat16 or wider, within the bound.
A program may use at most 128 MiB of HBM per device.

v0:
```python
import jax
import jax.numpy as jnp
from jax import lax
from jax.sharding import PartitionSpec as P

epsilon = 1e-06


def on_device(tapped, join_weight, norm_gain, cotangent, live_mask):
    full_rows = lax.all_gather(join_weight, "dp", axis=2, tiled=True)
    feature_count = full_rows.shape[2]
    combined = lax.psum_scatter(
        jnp.einsum("krc,ktr->ct", full_rows, tapped, preferred_element_type=jnp.float32).astype(
            jnp.bfloat16
        ),
        "weight",
        scatter_dimension=0,
        tiled=True,
    ).astype(jnp.float32)
    gain_column = norm_gain[:, None]
    wanted = cotangent.T.astype(jnp.float32) * live_mask[None, :].astype(jnp.float32)
    scaled = wanted * gain_column
    square_total = lax.psum(jnp.sum(combined * combined, axis=0), "weight")
    cross_total = lax.psum(jnp.sum(scaled * combined, axis=0), "weight")
    inverse = lax.rsqrt(square_total / feature_count + epsilon)
    projected = cross_total / feature_count
    hidden = (combined * inverse[None, :] * gain_column).T.astype(jnp.bfloat16)
    joined_grad = (
        inverse[None, :] * (scaled - combined * (inverse * inverse * projected)[None, :])
    ).astype(jnp.bfloat16)
    grad_term = jnp.einsum(
        "ktr,ct->krc",
        tapped,
        lax.all_gather(joined_grad, "weight", axis=0, tiled=True),
        preferred_element_type=jnp.float32,
    )
    gain_term = jnp.sum(wanted * combined * inverse[None, :], axis=1)
    grad_weight, grad_gain = (
        lax.psum(grad_term.astype(jnp.bfloat16), "dp").astype(jnp.float32),
        lax.psum(gain_term.astype(jnp.bfloat16), "dp").astype(jnp.float32),
    )
    return (hidden, grad_weight.astype(jnp.bfloat16), grad_gain)


def solution(mesh):
    return jax.shard_map(
        on_device,
        mesh=mesh,
        in_specs=(
            P(None, ("group", "dp"), "weight"),
            P(None, "weight", "dp"),
            P("weight"),
            P(("group", "dp"), "weight"),
            P(("group", "dp")),
        ),
        out_specs=(
            P(("group", "dp"), "weight"),
            P("group", "weight", None),
            P(("group", "weight")),
        ),
        check_vma=False,
    )
```

profile of v0, /device:TPU:17, one launch (start us, length us, event | category | flops | bytes accessed | tf_op | source)
XLA Modules:
  0.0 856.6 jit_solution(2238549716019024698)
XLA Ops:
  7.2 0.0 copy-start
  7.2 0.0 all-gather.3.cloned.1.call-start
  7.2 8.8 %copy.8 = bf16[3,1024,1024]{1,2,0:T(8,128)(2,1)} copy(bf16[3,1024,1024]{2,1,0:T(8,128)(2,1)} %param.6) | data formatting | bytes 12582912 | tf_op args[1]
  16.0 0.0 all-gather.3.cloned.1.call-update
  16.0 0.0 reduce-scatter.2.cloned.1.call-start
  16.1 156.4 %all-gather.3.cloned.1.call-done = bf16[3,1024,4096]{1,2,0:T(8,128)(2,1)} async-done(((bf16[3,1024,1024]{1,2,0:T(8,128)(2,1)}), bf16[3,1024,4096]{1,2,0:T(8,128)(2,1)}) %all-gather.3.cloned.1.call-update) | async-done | bytes 25165840 | tf_op jit(solution)/shard_map/all_gather | solution.py:10
  172.5 0.0 copy-done
  172.5 19.4 %bitcast_convert_fusion = bf16[4096,512]{1,0:T(8,128)(2,1)} fusion(bf16[3,1024,4096]{1,2,0:T(8,128)(2,1)} %all-gather.3.cloned.1.call-done, bf16[3,512,1024]{2,1,0:T(8,128)(2,1)S(1)} %copy-done), kind=kOutput, calls=%fused_computation.1 | convolution fusion | flops 12886999040 | bytes 32505856 | tf_op jit(solution)/shard_map/krc,ktr->ct/dot_general | solution.py:13
  191.9 0.0 copy-start.4
  191.9 0.0 reduce-scatter.2.cloned.1.call-update
  191.9 0.0 all-gather.5.cloned.1.call-start
  192.0 2.3 copy.9
  194.2 0.0 copy-done.4
  194.2 74.8 %reduce-scatter.2.cloned.1.call-done = bf16[1024,512]{1,0:T(8,128)(2,1)} async-done(((bf16[4096,512]{1,0:T(8,128)(2,1)}), bf16[1024,512]{1,0:T(8,128)(2,1)}) %reduce-scatter.2.cloned.1.call-update) | async-done | bytes 1048592 | tf_op jit(solution)/shard_map/reduce_scatter | solution.py:12
  269.0 1.5 fusion.1
  270.5 6.1 psum.28
  276.6 0.0 copy-done.3
  276.6 2.5 fusion.9
  279.1 7.0 psum.29
  286.1 3.6 fusion.7
  289.7 0.0 all-gather.5.cloned.1.call-update
  289.7 0.2 all-reduce.2.cloned.1.call-start
  290.0 84.7 %all-gather.5.cloned.1.call-done = bf16[4096,512]{1,0:T(8,128)(2,1)} async-done(((bf16[1024,512]{1,0:T(8,128)(2,1)}), bf16[4096,512]{1,0:T(8,128)(2,1)}) %all-gather.5.cloned.1.call-update) | async-done | bytes 4194320 | tf_op jit(solution)/shard_map/all_gather | solution.py:34
  374.7 19.2 %convert_bitcast_fusion = bf16[3,1024,4096]{1,2,0:T(8,128)(2,1)} fusion(bf16[3,512,1024]{2,1,0:T(8,128)(2,1)S(1)} %copy-done, bf16[4096,512]{1,0:T(8,128)(2,1)} %all-gather.5.cloned.1.call-done), kind=kOutput, calls=%fused_computation | convolution fusion | flops 12897484800 | bytes 32505856 | tf_op jit(solution)/shard_map/ktr,ct->krc/dot_general | solution.py:31
  393.9 0.0 all-reduce.2.cloned.1.call-update
  393.9 1.2 copy-done.2
  395.1 1.3 copy.10
  396.4 5.7 psum.31
  402.1 0.6 convert_element_type.47
  402.7 414.1 %all-reduce.2.cloned.1.call-done = bf16[3,1024,4096]{1,2,0:T(8,128)(2,1)} async-done(((bf16[3,1024,4096]{1,2,0:T(8,128)(2,1)}), bf16[3,1024,4096]{1,2,0:T(8,128)(2,1)}) %all-reduce.2.cloned.1.call-update) | async-done | bytes 25165840 | tf_op jit(solution)/shard_map/psum | solution.py:39
  816.7 33.3 %copy.11 = bf16[3,1024,4096]{2,1,0:T(8,128)(2,1)} copy(bf16[3,1024,4096]{1,2,0:T(8,128)(2,1)} %all-reduce.2.cloned.1.call-done) | data formatting | bytes 50331648
  850.1 0.0 copy-done.1
  (6 shorter events, 0.0 us)
Async XLA Ops:
  7.2 165.3 %copy-start = (bf16[3,512,1024]{2,1,0:T(8,128)(2,1)S(1)}, bf16[3,512,1024]{2,1,0:T(8,128)(2,1)}, u32[]{:S(2)}) copy-start(bf16[3,512,1024]{2,1,0:T(8,128)(2,1)} %param.5) | copy-start | bytes 9437188
  7.2 165.3 %all-gather.3.cloned.1.call-start = ((), (), s32[]{:S(2)}) async-start(), calls=%async_computation.1 | async-start | bytes 31457280 | tf_op jit(solution)/shard_map/all_gather | solution.py:10
  16.0 253.0 %reduce-scatter.2.cloned.1.call-start = ((), (), s32[]{:S(2)}) async-start(), calls=%async_computation.2 | async-start | bytes 5242880 | tf_op jit(solution)/shard_map/reduce_scatter | solution.py:12
  191.9 2.4 copy-start.4
  191.9 84.7 %copy-start.3 = (f32[1024]{0:T(1024)S(1)}, f32[1024]{0:T(1024)}, u32[]{:S(2)}) copy-start(f32[1024]{0:T(1024)} %param.7) | copy-start | bytes 12292
  191.9 182.8 %all-gather.5.cloned.1.call-start = ((), (), s32[]{:S(2)}) async-start(), calls=%async_computation.3 | async-start | bytes 5242880 | tf_op jit(solution)/shard_map/all_gather | solution.py:34
  289.7 527.0 %all-reduce.2.cloned.1.call-start = ((), (), s32[]{:S(2)}) async-start(), calls=%async_computation.4 | async-start | bytes 50331648 | tf_op jit(solution)/shard_map/psum | solution.py:39
  393.9 1.2 copy-start.2
  816.7 33.3 %copy-start.1 = (bf16[3,512,1024]{2,1,0:T(8,128)(2,1)S(1)}, bf16[3,512,1024]{2,1,0:T(8,128)(2,1)}, u32[]{:S(2)}) copy-start(bf16[3,512,1024]{2,1,0:T(8,128)(2,1)} %param.5) | copy-start | bytes 9437188
Sparse Core Ops, SparseCore 0:
  16.1 156.2 all-gather.2
  192.0 76.9 reduce-scatter.1
  289.9 84.7 all-gather.4
  394.0 422.6 all-reduce.1
where the time goes:
time: 860 us; the launch traced here: 857 us
  waiting for transfers between devices  730 us (85%)
  local copies, waits for them, and re-layouts  46.9 us (5%)
  matrix products  38.6 us (4%)
  blocking collectives  18.8 us (2%)
  between operations  13.8 us (2%)
    psum x1, waiting for transfers between devices, on_device(): lax.psum(grad_term.astype(jnp.bfloat16), 'dp').astype(jnp.float32)  414 us
    all_gather x1, waiting for transfers between devices, on_device(): full_rows = lax.all_gather(join_weight, 'dp', axis=2, tiled=True)  156 us
    all_gather x1, waiting for transfers between devices, on_device(): lax.all_gather(joined_grad, 'weight', axis=0, tiled=True)  84.7 us
    reduce_scatter x1, waiting for transfers between devices, on_device(): lax.psum_scatter(jnp.einsum('krc,ktr->ct', full_rows, tapped, preferred_e...  74.8 us
    unnamed x14, local copies, waits for them, and re-layouts  46.9 us
    dot_general x1, matrix products, on_device(): jnp.einsum('krc,ktr->ct', full_rows, tapped, preferred_element_type=jnp.f...  19.4 us
    dot_general x1, matrix products, on_device(): jnp.einsum('ktr,ct->krc', tapped, lax.all_gather(joined_grad, 'weight', a...  19.2 us
  transfers between devices with their start and end apart: 4, of which 4 were waited for; matrix products, arithmetic and copies ran while one was open for 0% of the time, Pallas kernels for 0%

commit v1 on v0

--- a/solution.py
+++ b/solution.py
@@ -1,9 +1,13 @@
+import functools
+
 import jax
 import jax.numpy as jnp
 from jax import lax
 from jax.sharding import PartitionSpec as P
 
 epsilon = 1e-06
+TOKEN_PARTS = 2
+COLUMN_PARTS = 2
 
 
 def on_device(tapped, join_weight, norm_gain, cotangent, live_mask):
@@ -42,9 +46,77 @@
     return (hidden, grad_weight.astype(jnp.bfloat16), grad_gain)
 
 
+def partner(count, flip):
+    return [(index, index ^ flip) for index in range(count)]
+
+
+def transposed(count):
+    return [(w * count + d, d * count + w) for w in range(count) for d in range(count)]
+
+
+def on_square(count, tapped, join_weight, norm_gain, cotangent, live_mask):
+    swap = transposed(count)
+    levels, tokens, rows = tapped.shape
+    columns = join_weight.shape[2]
+    feature_count = columns * count
+
+    def turn(block):
+        return lax.ppermute(block, ("weight", "dp"), swap)
+
+    wanted = turn(cotangent * live_mask[:, None].astype(cotangent.dtype)).astype(jnp.float32)
+    gain_row = turn(norm_gain)[None, :]
+    part = tokens // TOKEN_PARTS
+    gathered, pieces = [], []
+    for s in range(TOKEN_PARTS):
+        block = lax.all_gather(tapped[:, s * part : (s + 1) * part], "dp", axis=0)
+        gathered.append(block)
+        partial = jnp.einsum(
+            "dktr,krc->dtc", block, join_weight, preferred_element_type=jnp.float32
+        ).astype(jnp.bfloat16)
+        pieces.append(lax.psum_scatter(partial, "weight", scatter_dimension=0, tiled=False))
+    all_tapped = jnp.concatenate(gathered, axis=2)
+    combined = jnp.concatenate(pieces, axis=0).astype(jnp.float32)
+    scaled = wanted * gain_row
+    sums = lax.psum(
+        jnp.stack([jnp.sum(combined * combined, axis=1), jnp.sum(scaled * combined, axis=1)]), "dp"
+    )
+    inverse = lax.rsqrt(sums[0] / feature_count + epsilon)[:, None]
+    projected = (sums[1] / feature_count)[:, None]
+    joined_grad = (
+        inverse * (scaled - combined * (inverse * inverse * projected))
+    ).astype(jnp.bfloat16)
+    hidden = turn((combined * inverse * gain_row).astype(jnp.bfloat16))
+    gain_term = jnp.sum(wanted * combined * inverse, axis=0).astype(jnp.bfloat16)
+    grad_gain = turn(lax.psum(gain_term.astype(jnp.float32), "weight"))
+
+    me = lax.axis_index("dp")
+    width = columns // COLUMN_PARTS
+    grad_weight = jnp.zeros((levels, rows, feature_count), jnp.bfloat16)
+
+    def put(total, errors, owner, c):
+        term = jnp.einsum(
+            "dktr,dtc->krc", all_tapped, errors, preferred_element_type=jnp.float32
+        ).astype(jnp.bfloat16)
+        return lax.dynamic_update_slice(total, term, (0, 0, owner * columns + c * width))
+
+    mine = [
+        lax.all_gather(joined_grad[:, c * width : (c + 1) * width], "weight", axis=0)
+        for c in range(COLUMN_PARTS)
+    ]
+    far = [lax.ppermute(block, "dp", partner(count, 2)) for block in mine]
+    near = [lax.ppermute(block, "dp", partner(count, 1)) for block in mine]
+    last = [lax.ppermute(block, "dp", partner(count, 1)) for block in far]
+    for blocks, flip in ((mine, 0), (near, 1), (far, 2), (last, 3)):
+        for c, block in enumerate(blocks):
+            grad_weight = put(grad_weight, block, me ^ flip, c)
+    return (hidden, grad_weight, grad_gain)
+
+
 def solution(mesh):
+    count = mesh.shape["dp"]
+    square = count == 4 and mesh.shape["weight"] == count
     return jax.shard_map(
-        on_device,
+        functools.partial(on_square, count) if square else on_device,
         mesh=mesh,
         in_specs=(
             P(None, ("group", "dp"), "weight"),

time: 860 us -> 492 us (0.57)
  waiting for transfers between devices: 730 us -> 254 us
  blocking collectives: 18.8 us -> 87.8 us
  matrix products: 38.6 us -> 96 us
  local copies, waits for them, and re-layouts: 46.9 us -> 18.1 us
  starting transfers between devices: 0.35 us -> 17.3 us
    psum x1 -> x0, waiting for transfers between devices: 414 us -> none  [on_device(): lax.psum(grad_term.astype(jnp.bfloat16), 'dp').astype(jnp.float32)]
    all_gather x2 -> x4, waiting for transfers between devices: 241 us -> 118 us  [the longest x2 83.5 us: on_square(): block = lax.all_gather(tapped[:, s * part:(s + 1) * part], 'dp', axis=0)]
    ppermute x0 -> x10, waiting for transfers between devices: none -> 98.6 us  [the longest x4 73.9 us: turn(): return lax.ppermute(block, ('weight', 'dp'), swap)]
    psum x3 -> x2, blocking collectives: 18.8 us -> 87.8 us  [the longest x1 82.2 us: on_square(): grad_gain = turn(lax.psum(gain_term.astype(jnp.float32), 'weight'))]
    dot_general x2 -> x10, matrix products: 38.6 us -> 96 us  [the longest x8 72.8 us: put(): jnp.einsum('dktr,dtc->krc', all_tapped, errors, preferred_element_type=jn...]
    unnamed x14 -> x20, local copies, waits for them, and re-layouts: 46.9 us -> 1.6 us
    reduce_scatter x1 -> x2, waiting for transfers between devices: 74.8 us -> 36.5 us  [on_square(): lax.psum_scatter(partial, 'weight', scatter_dimension=0, tiled=False)]
    ppermute x0 -> x10, starting transfers between devices: none -> 17.1 us  [the longest x4 10.8 us: turn(): return lax.ppermute(block, ('weight', 'dp'), swap)]
  transfers between devices with their start and end apart: 4 -> 16, of which waited for: 4 -> 7; matrix products, arithmetic and copies ran while one was open for 0% -> 20% of each run, Pallas kernels for 0% -> 0%
where the time goes in v1:
time: 492 us
  waiting for transfers between devices  254 us (52%)
  matrix products  96 us (20%)
  blocking collectives  87.8 us (18%)
  local copies, waits for them, and re-layouts  18.1 us (4%)
  starting transfers between devices  17.3 us (4%)
  between operations  14.3 us (3%)
    all_gather x2, waiting for transfers between devices, on_square(): block = lax.all_gather(tapped[:, s * part:(s + 1) * part], 'dp', axis=0)  83.5 us
    psum x1, blocking collectives, on_square(): grad_gain = turn(lax.psum(gain_term.astype(jnp.float32), 'weight'))  82.2 us
    ppermute x4, waiting for transfers between devices, turn(): return lax.ppermute(block, ('weight', 'dp'), swap)  73.9 us
    dot_general x8, matrix products, put(): jnp.einsum('dktr,dtc->krc', all_tapped, errors, preferred_element_type=jn...  72.8 us
    reduce_scatter x2, waiting for transfers between devices, on_square(): lax.psum_scatter(partial, 'weight', scatter_dimension=0, tiled=False)  36.5 us
    all_gather x2, waiting for transfers between devices, on_square(): lax.all_gather(joined_grad[:, c * width:(c + 1) * width], 'weight', axis=0)  34.6 us
    ppermute x2, waiting for transfers between devices, on_square(): far = [lax.ppermute(block, 'dp', partner(count, 2)) for block in mine]  24.6 us
    dot_general x2, matrix products, on_square(): jnp.einsum('dktr,krc->dtc', block, join_weight, preferred_element_type=jn...  23.2 us
  transfers between devices with their start and end apart: 16, of which 7 were waited for; matrix products, arithmetic and copies ran while one was open for 20% of the time, Pallas kernels for 0%

profile of v1, /device:TPU:17, one launch (start us, length us, event | category | flops | bytes accessed | tf_op | source)
XLA Modules:
  0.0 492.1 jit_solution(16141171584471197910)
XLA Ops:
  7.2 4.2 fusion.33
  12.2 47.2 %all-gather.9.cloned.1.call-done = bf16[12,256,1024]{2,1,0:T(8,128)(2,1)} async-done(((bf16[3,256,1024]{2,1,0:T(8,128)(2,1)}), bf16[12,256,1024]{2,1,0:T(8,128)(2,1)}) %all-gather.9.cloned.1.call-update) | async-done | bytes 6291472 | tf_op jit(solution)/shard_map/all_gather | solution.py:71
  59.4 11.6 %bitcast_convert_fusion.9 = bf16[4,256,1024]{2,1,0:T(8,128)(2,1)} fusion(bf16[4,3,256,1024]{3,2,1,0:T(8,128)(2,1)} %bitcast.108, bf16[3,1024,1024]{2,1,0:T(8,128)(2,1)} %param.6), kind=kOutput, calls=%fused_computation.14 | convolution fusion | flops 6443499520 | bytes 14680064 | tf_op jit(solution)/shard_map/dktr,krc->dtc/dot_general | solution.py:73
  71.1 36.3 %all-gather.11.cloned.1.call-done = bf16[12,256,1024]{2,1,0:T(8,128)(2,1)} async-done(((bf16[3,256,1024]{2,1,0:T(8,128)(2,1)}), bf16[12,256,1024]{2,1,0:T(8,128)(2,1)}) %all-gather.11.cloned.1.call-update) | async-done | bytes 6291472 | tf_op jit(solution)/shard_map/all_gather | solution.py:71
  107.4 11.6 %bitcast_convert_fusion.8 = bf16[4,256,1024]{2,1,0:T(8,128)(2,1)} fusion(bf16[4,3,256,1024]{3,2,1,0:T(8,128)(2,1)} %bitcast.119, bf16[3,1024,1024]{2,1,0:T(8,128)(2,1)} %param.6), kind=kOutput, calls=%fused_computation.13 | convolution fusion | flops 6443499520 | bytes 14680064 | tf_op jit(solution)/shard_map/dktr,krc->dtc/dot_general | solution.py:73
  119.3 2.3 collective-permute-start
  121.6 4.2 collective-permute-start.1
  125.8 70.3 %collective-permute-done.1 = f32[1024]{0:T(1024)S(1)} collective-permute-done((f32[1024]{0:T(1024)S(1)}, f32[1024]{0:T(1024)S(1)}, u32[]{:S(2)}, u32[]{:S(2)}) %collective-permute-start.1) | collective-permute-done | bytes 4128 | tf_op jit(solution)/shard_map/ppermute | solution.py:64
  196.1 36.5 %reduce-scatter.5.cloned.1.call-done = bf16[1,256,1024]{2,1,0:T(8,128)(2,1)} async-done(((bf16[4,256,1024]{2,1,0:T(8,128)(2,1)}), bf16[1,256,1024]{2,1,0:T(8,128)(2,1)}) %reduce-scatter.5.cloned.1.call-update) | async-done | bytes 524304 | tf_op jit(solution)/shard_map/reduce_scatter | solution.py:76
  232.5 1.8 fusion.19
  234.3 5.6 %psum.14 = f32[2,512]{1,0:T(2,128)S(1)} all-reduce(f32[2,512]{1,0:T(2,128)S(1)} %pad_maximum_fusion.2), channel_id=1, replica_groups=mesh['group'=2,'weight'=4,'dp'=4] {'dp'}, use_global_device_ids=true, to_apply=%region_4.0 | all-reduce | flops 1024 | bytes 8192 | tf_op jit(solution)/shard_map/psum | solution.py:80
  240.0 2.1 fusion.24
  242.1 1.0 fusion.34
  243.7 2.3 collective-permute-start.2
  246.0 82.2 %psum.15 = f32[1024]{0:T(1024)S(1)} all-reduce(bf16[1024]{0:T(1024)(128)(2,1)S(1)} %get-tuple-element.7), channel_id=1, replica_groups=mesh['group'=2,'weight'=4,'dp'=4] {'weight'}, use_global_device_ids=true, to_apply=%region_6.0 | all-reduce | flops 1024 | bytes 6144 | tf_op jit(solution)/shard_map/psum | solution.py:90
  328.2 2.1 collective-permute-start.9
  330.3 3.7 collective-permute-done.9
  334.0 3.2 collective-permute-start.3
  337.2 34.6 %all-gather.15.cloned.1.call-done = bf16[2048,512]{1,0:T(8,128)(2,1)} async-done(((bf16[512,512]{1,0:T(8,128)(2,1)}), bf16[2048,512]{1,0:T(8,128)(2,1)}) %all-gather.15.cloned.1.call-update) | async-done | bytes 2097168 | tf_op jit(solution)/shard_map/all_gather | solution.py:103
  372.5 1.2 collective-permute-start.6
  373.7 11.3 %broadcast_in_dim.2 = bf16[3,1024,4096]{2,1,0:T(8,128)(2,1)} broadcast(bf16[]{:T(256)} %constant.10.clone.1), dimensions={} | broadcast | bytes 25165826 | tf_op jit(solution)/shard_map/broadcast_in_dim | solution.py:94
  385.1 11.2 %fusion.4 = bf16[3,1024,4096]{2,1,0:T(8,128)(2,1)} fusion(bf16[3,1024,4096]{2,1,0:T(8,128)(2,1)} %broadcast_in_dim.2, s32[]{:T(128)S(6)} %select_n.24, bf16[4,512,512,1]{2,1,3,0:T(8,128)(2,1)S(1)} %bitcast.132, bf16[4,3,256,1024]{3,2,1,0:T(8,128)(2,1)} %bitcast.120, bf16[4,3,256,1024]{3,2,1,0:T(8,128)(2,1)} %bitcast.109), kind=kOutput, calls=%fused_computation.20 | convolution fusion | flops 6469189632 | bytes 17825796 | tf_op jit(solution)/shard_map/dktr,dtc->krc/dot_general | solution.py:97
  396.3 8.4 %fusion.5 = bf16[3,1024,4096]{2,1,0:T(8,128)(2,1)} fusion(bf16[3,1024,4096]{2,1,0:T(8,128)(2,1)} %fusion.4, s32[]{:T(128)S(6)} %select_n.25, bf16[4,512,512,1]{2,1,3,0:T(8,128)(2,1)S(1)} %bitcast.135, bf16[4,3,256,1024]{3,2,1,0:T(8,128)(2,1)S(1)} %bitcast.123, bf16[4,3,256,1024]{3,2,1,0:T(8,128)(2,1)S(1)} %bitcast.112), kind=kOutput, calls=%fused_computation.21 | convolution fusion | flops 6469189632 | bytes 17825796 | tf_op jit(solution)/shard_map/dktr,dtc->krc/dot_general | solution.py:97
  404.9 24.6 %collective-permute-done.6 = bf16[4,512,512]{2,1,0:T(8,128)(2,1)S(1)} collective-permute-done((bf16[4,512,512]{2,1,0:T(8,128)(2,1)}, bf16[4,512,512]{2,1,0:T(8,128)(2,1)S(1)}, u32[]{:S(2)}, u32[]{:S(2)}) %collective-permute-start.6) | collective-permute-done | bytes 2097184 | tf_op jit(solution)/shard_map/ppermute | solution.py:106
  429.6 0.9 collective-permute-start.8
  430.4 9.9 %fusion.6 = bf16[3,1024,4096]{2,1,0:T(8,128)(2,1)} fusion(bf16[3,1024,4096]{2,1,0:T(8,128)(2,1)} %fusion.5, s32[]{:T(128)S(6)} %select_n.26, bf16[4,512,512]{2,1,0:T(8,128)(2,1)} %collective-permute-done.3, bf16[4,3,256,1024]{3,2,1,0:T(8,128)(2,1)S(1)} %bitcast.124, bf16[4,3,256,1024]{3,2,1,0:T(8,128)(2,1)S(1)} %bitcast.113), kind=kOutput, calls=%fused_computation.22 | convolution fusion | flops 6469189632 | bytes 17825796 | tf_op jit(solution)/shard_map/dktr,dtc->krc/dot_general | solution.py:97
  440.4 9.9 %fusion.7 = bf16[3,1024,4096]{2,1,0:T(8,128)(2,1)} fusion(bf16[3,1024,4096]{2,1,0:T(8,128)(2,1)} %fusion.6, s32[]{:T(128)S(6)} %select_n.27, bf16[4,512,512]{2,1,0:T(8,128)(2,1)} %collective-permute-done.4, bf16[4,3,256,1024]{3,2,1,0:T(8,128)(2,1)S(1)} %bitcast.125, bf16[4,3,256,1024]{3,2,1,0:T(8,128)(2,1)S(1)} %bitcast.114), kind=kOutput, calls=%fused_computation.23 | convolution fusion | flops 6469189632 | bytes 17825796 | tf_op jit(solution)/shard_map/dktr,dtc->krc/dot_general | solution.py:97
  450.3 8.3 %fusion.8 = bf16[3,1024,4096]{2,1,0:T(8,128)(2,1)} fusion(bf16[3,1024,4096]{2,1,0:T(8,128)(2,1)} %fusion.7, s32[]{:T(128)S(6)} %select_n.28, bf16[4,512,512]{2,1,0:T(8,128)(2,1)S(1)} %collective-permute-done.5, bf16[4,3,256,1024]{3,2,1,0:T(8,128)(2,1)S(1)} %bitcast.126, bf16[4,3,256,1024]{3,2,1,0:T(8,128)(2,1)S(1)} %bitcast.115), kind=kOutput, calls=%fused_computation.24 | convolution fusion | flops 6469189632 | bytes 17825796 | tf_op jit(solution)/shard_map/dktr,dtc->krc/dot_general | solution.py:97
  458.6 8.3 %fusion.9 = bf16[3,1024,4096]{2,1,0:T(8,128)(2,1)} fusion(bf16[3,1024,4096]{2,1,0:T(8,128)(2,1)} %fusion.8, s32[]{:T(128)S(6)} %select_n.29, bf16[4,512,512]{2,1,0:T(8,128)(2,1)S(1)} %collective-permute-done.6, bf16[4,3,256,1024]{3,2,1,0:T(8,128)(2,1)S(1)} %bitcast.127, bf16[4,3,256,1024]{3,2,1,0:T(8,128)(2,1)S(1)} %bitcast.116), kind=kOutput, calls=%fused_computation.25 | convolution fusion | flops 6469189632 | bytes 17825796 | tf_op jit(solution)/shard_map/dktr,dtc->krc/dot_general | solution.py:97
  467.0 8.3 %fusion.10 = bf16[3,1024,4096]{2,1,0:T(8,128)(2,1)} fusion(bf16[3,1024,4096]{2,1,0:T(8,128)(2,1)} %fusion.9, s32[]{:T(128)S(6)} %select_n.30, bf16[4,512,512]{2,1,0:T(8,128)(2,1)S(1)} %collective-permute-done.7, bf16[4,3,256,1024]{3,2,1,0:T(8,128)(2,1)S(1)} %bitcast.128, bf16[4,3,256,1024]{3,2,1,0:T(8,128)(2,1)S(1)} %bitcast.117), kind=kOutput, calls=%fused_computation.26 | convolution fusion | flops 6469189632 | bytes 17825796 | tf_op jit(solution)/shard_map/dktr,dtc->krc/dot_general | solution.py:97
  475.3 8.3 %fusion.11 = bf16[3,1024,4096]{2,1,0:T(8,128)(2,1)} fusion(bf16[3,1024,4096]{2,1,0:T(8,128)(2,1)} %fusion.10, s32[]{:T(128)S(6)} %select_n.31, bf16[4,512,512]{2,1,0:T(8,128)(2,1)S(1)} %collective-permute-done.8, bf16[4,3,256,1024]{3,2,1,0:T(8,128)(2,1)S(1)} %bitcast.129, bf16[4,3,256,1024]{3,2,1,0:T(8,128)(2,1)S(1)} %bitcast.118), kind=kOutput, calls=%fused_computation.27 | convolution fusion | flops 6469189632 | bytes 17825796 | tf_op jit(solution)/shard_map/dktr,dtc->krc/dot_general | solution.py:97
  483.7 1.0 copy.52
  (50 shorter events, 3.3 us)
Async XLA Ops:
  7.2 52.3 %all-gather.9.cloned.1.call-start = ((), (), s32[]{:S(2)}) async-start(), calls=%async_computation.4 | async-start | bytes 7864320 | tf_op jit(solution)/shard_map/all_gather | solution.py:71
  11.4 96.0 %all-gather.11.cloned.1.call-start = ((), (), s32[]{:S(2)}) async-start(), calls=%async_computation.5 | async-start | bytes 7864320 | tf_op jit(solution)/shard_map/all_gather | solution.py:71
  12.1 183.9 %reduce-scatter.3.cloned.1.call-start = ((), (), s32[]{:S(2)}) async-start(), calls=%async_computation.2 | async-start | bytes 2621440 | tf_op jit(solution)/shard_map/reduce_scatter | solution.py:76
  71.0 161.5 %reduce-scatter.5.cloned.1.call-start = ((), (), s32[]{:S(2)}) async-start(), calls=%async_computation.3 | async-start | bytes 2621440 | tf_op jit(solution)/shard_map/reduce_scatter | solution.py:76
  107.4 11.7 %copy-start.1 = (s32[512]{0:T(512)S(1)}, s32[512]{0:T(512)}, u32[]{:S(2)}) copy-start(s32[512]{0:T(512)} %param.9) | copy-start | bytes 6148
  107.4 11.7 %copy-start = (bf16[512,1024]{1,0:T(8,128)(2,1)S(1)}, bf16[512,1024]{1,0:T(8,128)(2,1)}, u32[]{:S(2)}) copy-start(bf16[512,1024]{1,0:T(8,128)(2,1)} %param.8) | copy-start | bytes 3145732
  107.4 14.2 %copy-start.4 = (f32[1024]{0:T(1024)S(1)}, f32[1024]{0:T(1024)}, u32[]{:S(2)}) copy-start(f32[1024]{0:T(1024)} %param.7) | copy-start | bytes 12292
  119.1 215.0 %all-gather.13.cloned.1.call-start = ((), (), s32[]{:S(2)}) async-start(), calls=%async_computation.6 | async-start | bytes 2621440 | tf_op jit(solution)/shard_map/all_gather | solution.py:103
  119.3 76.8 %collective-permute-start = (bf16[512,1024]{1,0:T(8,128)(2,1)S(1)}, bf16[512,1024]{1,0:T(8,128)(2,1)S(1)}, u32[]{:S(2)}, u32[]{:S(2)}) collective-permute-start(bf16[512,1024]{1,0:T(8,128)(2,1)S(1)} %broadcast_multiply_fusion), channel_id=1, source_target_pairs={{0,0},{1,4},{2,8},{3,12},{4,1},{5,5},{6,9},{7,13},{8,2},{9,6},{10,... | collective-permute-start | bytes 3145736 | tf_op jit(solution)/shard_map/ppermute | solution.py:64
  121.6 74.5 %collective-permute-start.1 = (f32[1024]{0:T(1024)S(1)}, f32[1024]{0:T(1024)S(1)}, u32[]{:S(2)}, u32[]{:S(2)}) collective-permute-start(f32[1024]{0:T(1024)S(1)} %copy-done.4), channel_id=1, source_target_pairs={{0,0},{1,4},{2,8},{3,12},{4,1},{5,5},{6,9},{7,13},{8,2},{9,6},{10,... | collective-permute-start | bytes 12296 | tf_op jit(solution)/shard_map/ppermute | solution.py:64
  243.2 128.7 %all-gather.15.cloned.1.call-start = ((), (), s32[]{:S(2)}) async-start(), calls=%async_computation.7 | async-start | bytes 2621440 | tf_op jit(solution)/shard_map/all_gather | solution.py:103
  243.7 90.3 %collective-permute-start.2 = (bf16[512,1024]{1,0:T(8,128)(2,1)S(1)}, bf16[512,1024]{1,0:T(8,128)(2,1)S(1)}, u32[]{:S(2)}, u32[]{:S(2)}) collective-permute-start(bf16[512,1024]{1,0:T(8,128)(2,1)S(1)} %get-tuple-element.9), channel_id=1, source_target_pairs={{0,0},{1,4},{2,8},{3,12},{4,1},{5,5},{6,9},{7,13},{8,2},{9,6},{10,... | collective-permute-start | bytes 3145736 | tf_op jit(solution)/shard_map/ppermute | solution.py:64
  328.2 5.8 %collective-permute-start.9 = (f32[1024]{0:T(1024)S(1)}, f32[1024]{0:T(1024)S(1)}, u32[]{:S(2)}, u32[]{:S(2)}) collective-permute-start(f32[1024]{0:T(1024)S(1)} %psum.15), channel_id=1, source_target_pairs={{0,0},{1,4},{2,8},{3,12},{4,1},{5,5},{6,9},{7,13},{8,2},{9,6},{10,... | collective-permute-start | bytes 12296 | tf_op jit(solution)/shard_map/ppermute | solution.py:64
  334.0 96.4 %collective-permute-start.3 = (bf16[4,512,512]{2,1,0:T(8,128)(2,1)}, bf16[4,512,512]{2,1,0:T(8,128)(2,1)}, u32[]{:S(2)}, u32[]{:S(2)}) collective-permute-start(bf16[4,512,512]{2,1,0:T(8,128)(2,1)} %bitcast.130), channel_id=1, source_target_pairs={{0,1},{1,0},{2,3},{3,2},{4,5},{5,4},{6,7},{7,6},{8,9},{9,8},{10,11... | collective-permute-start | bytes 6291464 | tf_op jit(solution)/shard_map/ppermute | solution.py:107
  337.2 67.4 %collective-permute-start.5 = (bf16[4,512,512]{2,1,0:T(8,128)(2,1)}, bf16[4,512,512]{2,1,0:T(8,128)(2,1)S(1)}, u32[]{:S(2)}, u32[]{:S(2)}) collective-permute-start(bf16[4,512,512]{2,1,0:T(8,128)(2,1)} %bitcast.131), channel_id=1, source_target_pairs={{0,2},{1,3},{2,0},{3,1},{4,6},{5,7},{6,4},{7,5},{8,10},{9,11},{10,... | collective-permute-start | bytes 6291464 | tf_op jit(solution)/shard_map/ppermute | solution.py:106
  371.8 68.5 %collective-permute-start.4 = (bf16[4,512,512]{2,1,0:T(8,128)(2,1)}, bf16[4,512,512]{2,1,0:T(8,128)(2,1)}, u32[]{:S(2)}, u32[]{:S(2)}) collective-permute-start(bf16[4,512,512]{2,1,0:T(8,128)(2,1)} %bitcast.133), channel_id=1, source_target_pairs={{0,1},{1,0},{2,3},{3,2},{4,5},{5,4},{6,7},{7,6},{8,9},{9,8},{10,11... | collective-permute-start | bytes 6291464 | tf_op jit(solution)/shard_map/ppermute | solution.py:107
  372.5 57.1 %collective-permute-start.6 = (bf16[4,512,512]{2,1,0:T(8,128)(2,1)}, bf16[4,512,512]{2,1,0:T(8,128)(2,1)S(1)}, u32[]{:S(2)}, u32[]{:S(2)}) collective-permute-start(bf16[4,512,512]{2,1,0:T(8,128)(2,1)} %bitcast.134), channel_id=1, source_target_pairs={{0,2},{1,3},{2,0},{3,1},{4,6},{5,7},{6,4},{7,5},{8,10},{9,11},{10,... | collective-permute-start | bytes 6291464 | tf_op jit(solution)/shard_map/ppermute | solution.py:106
  373.7 11.3 %copy-start.2 = (bf16[2048,512]{1,0:T(8,128)(2,1)S(1)}, bf16[2048,512]{1,0:T(8,128)(2,1)}, u32[]{:S(2)}) copy-start(bf16[2048,512]{1,0:T(8,128)(2,1)} %all-gather.13.cloned.1.call-done) | copy-start | bytes 6291460
  373.7 22.5 %slice-start = ((s8[6291456]{0:T(1024)(128)(4,1)}), s8[4194304]{0:T(1024)(128)(4,1)S(1)}, s32[]{:S(2)}) async-start(s8[6291456]{0:T(1024)(128)(4,1)} %bitcast.110), calls=%async_computation.8 | async-start | bytes 8388608
  373.7 22.5 %slice-start.2 = ((s8[6291456]{0:T(1024)(128)(4,1)}), s8[4194304]{0:T(1024)(128)(4,1)S(1)}, s32[]{:S(2)}) async-start(s8[6291456]{0:T(1024)(128)(4,1)} %bitcast.121), calls=%async_computation.10 | async-start | bytes 8388608
  385.0 11.2 %slice-start.1 = ((s8[6291456]{0:T(1024)(128)(4,1)}), s8[2097152]{0:T(1024)(128)(4,1)S(1)}, s32[]{:S(2)}) async-start(s8[6291456]{0:T(1024)(128)(4,1)} %bitcast.110), calls=%async_computation.9 | async-start | bytes 4194304
  385.0 11.2 %slice-start.3 = ((s8[6291456]{0:T(1024)(128)(4,1)}), s8[2097152]{0:T(1024)(128)(4,1)S(1)}, s32[]{:S(2)}) async-start(s8[6291456]{0:T(1024)(128)(4,1)} %bitcast.121), calls=%async_computation.11 | async-start | bytes 4194304
  385.0 11.2 %copy-start.3 = (bf16[2048,512]{1,0:T(8,128)(2,1)S(1)}, bf16[2048,512]{1,0:T(8,128)(2,1)}, u32[]{:S(2)}) copy-start(bf16[2048,512]{1,0:T(8,128)(2,1)} %all-gather.15.cloned.1.call-done) | copy-start | bytes 6291460
  404.7 62.3 %collective-permute-start.7 = (bf16[4,512,512]{2,1,0:T(8,128)(2,1)S(1)}, bf16[4,512,512]{2,1,0:T(8,128)(2,1)S(1)}, u32[]{:S(2)}, u32[]{:S(2)}) collective-permute-start(bf16[4,512,512]{2,1,0:T(8,128)(2,1)S(1)} %collective-permute-done.5), channel_id=1, source_target_pairs={{0,1},{1,0},{2,3},{3,2},{4,5},{5,4},{6,7},{7,6},{8,9},{9,8},{10,11... | collective-permute-start | bytes 6291464 | tf_op jit(solution)/shard_map/ppermute | solution.py:108
  429.6 45.7 %collective-permute-start.8 = (bf16[4,512,512]{2,1,0:T(8,128)(2,1)S(1)}, bf16[4,512,512]{2,1,0:T(8,128)(2,1)S(1)}, u32[]{:S(2)}, u32[]{:S(2)}) collective-permute-start(bf16[4,512,512]{2,1,0:T(8,128)(2,1)S(1)} %collective-permute-done.6), channel_id=1, source_target_pairs={{0,1},{1,0},{2,3},{3,2},{4,5},{5,4},{6,7},{7,6},{8,9},{9,8},{10,11... | collective-permute-start | bytes 6291464 | tf_op jit(solution)/shard_map/ppermute | solution.py:108
Sparse Core Ops, SparseCore 0:
  11.5 47.8 all-gather.8
  61.0 46.3 all-gather.10
  109.7 76.1 reduce-scatter.2
  188.7 43.8 reduce-scatter.4
  243.3 76.7 all-gather.12
  322.0 49.7 all-gather.14

commit v2 on v1

--- a/solution.py
+++ b/solution.py
@@ -63,12 +63,14 @@
     def turn(block):
         return lax.ppermute(block, ("weight", "dp"), swap)
 
-    wanted = turn(cotangent * live_mask[:, None].astype(cotangent.dtype)).astype(jnp.float32)
+    wanted = turn(cotangent * live_mask[:, None].astype(cotangent.dtype))
     gain_row = turn(norm_gain)[None, :]
     part = tokens // TOKEN_PARTS
     gathered, pieces = [], []
     for s in range(TOKEN_PARTS):
         block = lax.all_gather(tapped[:, s * part : (s + 1) * part], "dp", axis=0)
+        if s == 0:
+            block, wanted, gain_row = lax.optimization_barrier((block, wanted, gain_row))
         gathered.append(block)
         partial = jnp.einsum(
             "dktr,krc->dtc", block, join_weight, preferred_element_type=jnp.float32
@@ -76,6 +78,7 @@
         pieces.append(lax.psum_scatter(partial, "weight", scatter_dimension=0, tiled=False))
     all_tapped = jnp.concatenate(gathered, axis=2)
     combined = jnp.concatenate(pieces, axis=0).astype(jnp.float32)
+    wanted = wanted.astype(jnp.float32)
     scaled = wanted * gain_row
     sums = lax.psum(
         jnp.stack([jnp.sum(combined * combined, axis=1), jnp.sum(scaled * combined, axis=1)]), "dp"
@@ -85,9 +88,8 @@
     joined_grad = (
         inverse * (scaled - combined * (inverse * inverse * projected))
     ).astype(jnp.bfloat16)
-    hidden = turn((combined * inverse * gain_row).astype(jnp.bfloat16))
+    normed = (combined * inverse * gain_row).astype(jnp.bfloat16)
     gain_term = jnp.sum(wanted * combined * inverse, axis=0).astype(jnp.bfloat16)
-    grad_gain = turn(lax.psum(gain_term.astype(jnp.float32), "weight"))
 
     me = lax.axis_index("dp")
     width = columns // COLUMN_PARTS
@@ -103,9 +105,13 @@
         lax.all_gather(joined_grad[:, c * width : (c + 1) * width], "weight", axis=0)
         for c in range(COLUMN_PARTS)
     ]
+    mine[-1], normed = lax.optimization_barrier((mine[-1], normed))
     far = [lax.ppermute(block, "dp", partner(count, 2)) for block in mine]
+    far[0], gain_term = lax.optimization_barrier((far[0], gain_term))
     near = [lax.ppermute(block, "dp", partner(count, 1)) for block in mine]
     last = [lax.ppermute(block, "dp", partner(count, 1)) for block in far]
+    hidden = turn(normed)
+    grad_gain = turn(lax.psum(gain_term.astype(jnp.float32), "weight"))
     for blocks, flip in ((mine, 0), (near, 1), (far, 2), (last, 3)):
         for c, block in enumerate(blocks):
             grad_weight = put(grad_weight, block, me ^ flip, c)

time: 492 us -> 460 us (0.935)
  blocking collectives: 87.8 us -> 12.4 us
  waiting for transfers between devices: 254 us -> 286 us
  matrix products: 96 us -> 104 us
    psum x1, blocking collectives: 82.2 us -> 6.78 us  [on_square(): grad_gain = turn(lax.psum(gain_term.astype(jnp.float32), 'weight'))]
    all_gather x2, waiting for transfers between devices: 34.6 us -> 89.2 us  [on_square(): lax.all_gather(joined_grad[:, c * width:(c + 1) * width], 'weight', axis=0)]
    reduce_scatter x2, waiting for transfers between devices: 36.5 us -> 79.5 us  [on_square(): lax.psum_scatter(partial, 'weight', scatter_dimension=0, tiled=False)]
    all_gather x2, waiting for transfers between devices: 83.5 us -> 55.3 us  [on_square(): block = lax.all_gather(tapped[:, s * part:(s + 1) * part], 'dp', axis=0)]
    ppermute x2, waiting for transfers between devices: 24.6 us -> 0.01 us  [on_square(): far = [lax.ppermute(block, 'dp', partner(count, 2)) for block in mine]]
    ppermute x4, waiting for transfers between devices: 73.9 us -> 61.1 us  [turn(): return lax.ppermute(block, ('weight', 'dp'), swap)]
    dot_general x8, matrix products: 72.8 us -> 81.2 us  [put(): jnp.einsum('dktr,dtc->krc', all_tapped, errors, preferred_element_type=jn...]
  transfers between devices with their start and end apart: 16 -> 16, of which waited for: 7 -> 8; matrix products, arithmetic and copies ran while one was open for 20% -> 24% of each run, Pallas kernels for 0% -> 0%
where the time goes in v2:
time: 460 us; the launch traced here: 458 us
  waiting for transfers between devices  286 us (62%)
  matrix products  104 us (23%)
  starting transfers between devices  18.3 us (4%)
  local copies, waits for them, and re-layouts  18.1 us (4%)
  between operations  14.4 us (3%)
  blocking collectives  12.4 us (3%)
    all_gather x2, waiting for transfers between devices, on_square(): lax.all_gather(joined_grad[:, c * width:(c + 1) * width], 'weight', axis=0)  89.2 us
    dot_general x8, matrix products, put(): jnp.einsum('dktr,dtc->krc', all_tapped, errors, preferred_element_type=jn...  81.2 us
    reduce_scatter x2, waiting for transfers between devices, on_square(): lax.psum_scatter(partial, 'weight', scatter_dimension=0, tiled=False)  79.5 us
    ppermute x4, waiting for transfers between devices, turn(): return lax.ppermute(block, ('weight', 'dp'), swap)  61.1 us
    all_gather x2, waiting for transfers between devices, on_square(): block = lax.all_gather(tapped[:, s * part:(s + 1) * part], 'dp', axis=0)  55.3 us
    dot_general x2, matrix products, on_square(): jnp.einsum('dktr,krc->dtc', block, join_weight, preferred_element_type=jn...  23.3 us
    ppermute x4, starting transfers between devices, turn(): return lax.ppermute(block, ('weight', 'dp'), swap)  14.3 us
    broadcast_in_dim x1, local copies, waits for them, and re-layouts, on_square(): grad_weight = jnp.zeros((levels, rows, feature_count), jnp.bfloat16)  11.3 us
  transfers between devices with their start and end apart: 16, of which 8 were waited for; matrix products, arithmetic and copies ran while one was open for 24% of the time, Pallas kernels for 0%

profile of v2, /device:TPU:17, one launch (start us, length us, event | category | flops | bytes accessed | tf_op | source)
XLA Modules:
  0.0 458.1 jit_solution(9972271878491816579)
XLA Ops:
  7.2 4.1 fusion.34
  12.2 47.2 %all-gather.11.cloned.1.call-done = bf16[12,256,1024]{2,1,0:T(8,128)(2,1)} async-done(((bf16[3,256,1024]{2,1,0:T(8,128)(2,1)}), bf16[12,256,1024]{2,1,0:T(8,128)(2,1)}) %all-gather.11.cloned.1.call-update) | async-done | bytes 6291472 | tf_op jit(solution)/shard_map/all_gather | solution.py:71
  59.4 11.6 %bitcast_convert_fusion.8 = bf16[4,256,1024]{2,1,0:T(8,128)(2,1)} fusion(bf16[4,3,256,1024]{3,2,1,0:T(8,128)(2,1)} %bitcast.110, bf16[3,1024,1024]{2,1,0:T(8,128)(2,1)} %param.6), kind=kOutput, calls=%fused_computation.13 | convolution fusion | flops 6443499520 | bytes 14680064 | tf_op jit(solution)/shard_map/dktr,krc->dtc/dot_general | solution.py:75
  71.3 2.3 collective-permute-start
  73.6 4.2 collective-permute-start.1
  77.8 44.1 %collective-permute-done.1 = f32[1024]{0:T(1024)S(1)} collective-permute-done((f32[1024]{0:T(1024)S(1)}, f32[1024]{0:T(1024)S(1)}, u32[]{:S(2)}, u32[]{:S(2)}) %collective-permute-start.1) | collective-permute-done | bytes 4128 | tf_op jit(solution)/shard_map/ppermute | solution.py:64
  121.9 8.1 %all-gather.9.cloned.1.call-done = bf16[12,256,1024]{2,1,0:T(8,128)(2,1)} async-done(((bf16[3,256,1024]{2,1,0:T(8,128)(2,1)}), bf16[12,256,1024]{2,1,0:T(8,128)(2,1)}) %all-gather.9.cloned.1.call-update) | async-done | bytes 6291472 | tf_op jit(solution)/shard_map/all_gather | solution.py:71
  129.9 11.6 %bitcast_convert_fusion.9 = bf16[4,256,1024]{2,1,0:T(8,128)(2,1)} fusion(bf16[4,3,256,1024]{3,2,1,0:T(8,128)(2,1)} %bitcast.123, bf16[3,1024,1024]{2,1,0:T(8,128)(2,1)} %param.6), kind=kOutput, calls=%fused_computation.14 | convolution fusion | flops 6443499520 | bytes 14680064 | tf_op jit(solution)/shard_map/dktr,krc->dtc/dot_general | solution.py:75
  141.6 34.0 %reduce-scatter.5.cloned.1.call-done = bf16[1,256,1024]{2,1,0:T(8,128)(2,1)} async-done(((bf16[4,256,1024]{2,1,0:T(8,128)(2,1)}), bf16[1,256,1024]{2,1,0:T(8,128)(2,1)}) %reduce-scatter.5.cloned.1.call-update) | async-done | bytes 524304 | tf_op jit(solution)/shard_map/reduce_scatter | solution.py:78
  175.7 45.5 %reduce-scatter.3.cloned.1.call-done = bf16[1,256,1024]{2,1,0:T(8,128)(2,1)} async-done(((bf16[4,256,1024]{2,1,0:T(8,128)(2,1)}), bf16[1,256,1024]{2,1,0:T(8,128)(2,1)}) %reduce-scatter.3.cloned.1.call-update) | async-done | bytes 524304 | tf_op jit(solution)/shard_map/reduce_scatter | solution.py:78
  221.1 1.8 fusion.19
  222.9 5.6 %psum.14 = f32[2,512]{1,0:T(2,128)S(1)} all-reduce(f32[2,512]{1,0:T(2,128)S(1)} %pad_maximum_fusion.2), channel_id=1, replica_groups=mesh['group'=2,'weight'=4,'dp'=4] {'dp'}, use_global_device_ids=true, to_apply=%region_4.0 | all-reduce | flops 1024 | bytes 8192 | tf_op jit(solution)/shard_map/psum | solution.py:83
  228.6 2.1 fusion.24
  230.7 1.0 fusion.35
  232.4 44.3 %all-gather.15.cloned.1.call-done = bf16[2048,512]{1,0:T(8,128)(2,1)} async-done(((bf16[512,512]{1,0:T(8,128)(2,1)}), bf16[2048,512]{1,0:T(8,128)(2,1)}) %all-gather.15.cloned.1.call-update) | async-done | bytes 2097168 | tf_op jit(solution)/shard_map/all_gather | solution.py:105
  277.4 1.2 collective-permute-start.5
  278.6 44.8 %all-gather.13.cloned.1.call-done = bf16[2048,512]{1,0:T(8,128)(2,1)} async-done(((bf16[512,512]{1,0:T(8,128)(2,1)}), bf16[2048,512]{1,0:T(8,128)(2,1)}) %all-gather.13.cloned.1.call-update) | async-done | bytes 2097168 | tf_op jit(solution)/shard_map/all_gather | solution.py:105
  324.1 1.2 collective-permute-start.6
  325.3 2.3 collective-permute-start.2
  327.6 11.3 %broadcast_in_dim.10 = bf16[3,1024,4096]{2,1,0:T(8,128)(2,1)} broadcast(bf16[]{:T(256)} %constant.10.clone.1), dimensions={} | broadcast | bytes 25165826 | tf_op jit(solution)/shard_map/broadcast_in_dim | solution.py:96
  338.9 11.2 %fusion.4 = bf16[3,1024,4096]{2,1,0:T(8,128)(2,1)} fusion(bf16[3,1024,4096]{2,1,0:T(8,128)(2,1)} %broadcast_in_dim.10, s32[]{:T(128)S(6)} %select_n.24, bf16[4,512,512,1]{2,1,3,0:T(8,128)(2,1)S(1)} %bitcast.141, bf16[4,3,256,1024]{3,2,1,0:T(8,128)(2,1)} %bitcast.111, bf16[4,3,256,1024]{3,2,1,0:T(8,128)(2,1)} %bitcast.124), kind=kOutput, calls=%fused_computation.20 | convolution fusion | flops 6469189632 | bytes 17825796 | tf_op jit(solution)/shard_map/dktr,dtc->krc/dot_general | solution.py:99
  350.2 8.4 %fusion.5 = bf16[3,1024,4096]{2,1,0:T(8,128)(2,1)} fusion(bf16[3,1024,4096]{2,1,0:T(8,128)(2,1)} %fusion.4, s32[]{:T(128)S(6)} %select_n.25, bf16[4,512,512]{2,1,0:T(8,128)(2,1)S(1)} %bitcast.138, bf16[4,3,256,1024]{3,2,1,0:T(8,128)(2,1)S(1)} %bitcast.116, bf16[4,3,256,1024]{3,2,1,0:T(8,128)(2,1)S(1)} %bitcast.129), kind=kOutput, calls=%fused_computation.21 | convolution fusion | flops 6469189632 | bytes 17825796 | tf_op jit(solution)/shard_map/dktr,dtc->krc/dot_general | solution.py:99
  358.5 17.1 %collective-permute-done.2 = bf16[512,1024]{1,0:T(8,128)(2,1)S(1)} collective-permute-done((bf16[512,1024]{1,0:T(8,128)(2,1)S(1)}, bf16[512,1024]{1,0:T(8,128)(2,1)S(1)}, u32[]{:S(2)}, u32[]{:S(2)}) %collective-permute-start.2) | collective-permute-done | bytes 1048608 | tf_op jit(solution)/shard_map/ppermute | solution.py:64
  375.6 6.8 %psum.15 = f32[1024]{0:T(1024)S(1)} all-reduce(bf16[1024]{0:T(1024)(128)(2,1)S(1)} %get-tuple-element.16), channel_id=1, replica_groups=mesh['group'=2,'weight'=4,'dp'=4] {'weight'}, use_global_device_ids=true, to_apply=%region_6.0 | all-reduce | flops 1024 | bytes 6144 | tf_op jit(solution)/shard_map/psum | solution.py:114
  382.4 5.6 %collective-permute-start.9 = (f32[1024]{0:T(1024)S(1)}, f32[1024]{0:T(1024)S(1)}, u32[]{:S(2)}, u32[]{:S(2)}) collective-permute-start(f32[1024]{0:T(1024)S(1)} %psum.15), channel_id=1, source_target_pairs={{0,0},{1,4},{2,8},{3,12},{4,1},{5,5},{6,9},{7,13},{8,2},{9,6},{10,... | collective-permute-start | bytes 12296 | tf_op jit(solution)/shard_map/ppermute | solution.py:64
  388.0 12.0 %fusion.6 = bf16[3,1024,4096]{2,1,0:T(8,128)(2,1)} fusion(bf16[3,1024,4096]{2,1,0:T(8,128)(2,1)} %fusion.5, s32[]{:T(128)S(6)} %select_n.26, bf16[4,512,512]{2,1,0:T(8,128)(2,1)} %collective-permute-done.3, bf16[4,3,256,1024]{3,2,1,0:T(8,128)(2,1)} %bitcast.112, bf16[4,3,256,1024]{3,2,1,0:T(8,128)(2,1)} %bitcast.125), kind=kOutput, calls=%fused_computation.22 | convolution fusion | flops 6469189632 | bytes 17825796 | tf_op jit(solution)/shard_map/dktr,dtc->krc/dot_general | solution.py:99
  400.0 11.7 %fusion.7 = bf16[3,1024,4096]{2,1,0:T(8,128)(2,1)} fusion(bf16[3,1024,4096]{2,1,0:T(8,128)(2,1)} %fusion.6, s32[]{:T(128)S(6)} %select_n.27, bf16[4,512,512]{2,1,0:T(8,128)(2,1)} %collective-permute-done.4, bf16[4,3,256,1024]{3,2,1,0:T(8,128)(2,1)} %bitcast.113, bf16[4,3,256,1024]{3,2,1,0:T(8,128)(2,1)} %bitcast.126), kind=kOutput, calls=%fused_computation.23 | convolution fusion | flops 6469189632 | bytes 17825796 | tf_op jit(solution)/shard_map/dktr,dtc->krc/dot_general | solution.py:99
  411.8 9.8 %fusion.8 = bf16[3,1024,4096]{2,1,0:T(8,128)(2,1)} fusion(bf16[3,1024,4096]{2,1,0:T(8,128)(2,1)} %fusion.7, s32[]{:T(128)S(6)} %select_n.28, bf16[4,512,512]{2,1,0:T(8,128)(2,1)} %collective-permute-done.5, bf16[4,3,256,1024]{3,2,1,0:T(8,128)(2,1)S(1)} %bitcast.119, bf16[4,3,256,1024]{3,2,1,0:T(8,128)(2,1)S(1)} %bitcast.132), kind=kOutput, calls=%fused_computation.24 | convolution fusion | flops 6469189632 | bytes 17825796 | tf_op jit(solution)/shard_map/dktr,dtc->krc/dot_general | solution.py:99
  421.6 9.8 %fusion.9 = bf16[3,1024,4096]{2,1,0:T(8,128)(2,1)} fusion(bf16[3,1024,4096]{2,1,0:T(8,128)(2,1)} %fusion.8, s32[]{:T(128)S(6)} %select_n.29, bf16[4,512,512]{2,1,0:T(8,128)(2,1)} %collective-permute-done.6, bf16[4,3,256,1024]{3,2,1,0:T(8,128)(2,1)S(1)} %bitcast.120, bf16[4,3,256,1024]{3,2,1,0:T(8,128)(2,1)S(1)} %bitcast.133), kind=kOutput, calls=%fused_computation.25 | convolution fusion | flops 6469189632 | bytes 17825796 | tf_op jit(solution)/shard_map/dktr,dtc->krc/dot_general | solution.py:99
  431.4 10.1 %fusion.10 = bf16[3,1024,4096]{2,1,0:T(8,128)(2,1)} fusion(bf16[3,1024,4096]{2,1,0:T(8,128)(2,1)} %fusion.9, s32[]{:T(128)S(6)} %select_n.30, bf16[4,512,512]{2,1,0:T(8,128)(2,1)} %collective-permute-done.7, bf16[4,3,256,1024]{3,2,1,0:T(8,128)(2,1)S(1)} %bitcast.121, bf16[4,3,256,1024]{3,2,1,0:T(8,128)(2,1)S(1)} %bitcast.134), kind=kOutput, calls=%fused_computation.26 | convolution fusion | flops 6469189632 | bytes 17825796 | tf_op jit(solution)/shard_map/dktr,dtc->krc/dot_general | solution.py:99
  441.5 8.2 %fusion.11 = bf16[3,1024,4096]{2,1,0:T(8,128)(2,1)} fusion(bf16[3,1024,4096]{2,1,0:T(8,128)(2,1)} %fusion.10, s32[]{:T(128)S(6)} %select_n.31, bf16[4,512,512]{2,1,0:T(8,128)(2,1)S(1)} %collective-permute-done.8, bf16[4,3,256,1024]{3,2,1,0:T(8,128)(2,1)S(1)} %bitcast.122, bf16[4,3,256,1024]{3,2,1,0:T(8,128)(2,1)S(1)} %bitcast.135), kind=kOutput, calls=%fused_computation.27 | convolution fusion | flops 6469189632 | bytes 17825796 | tf_op jit(solution)/shard_map/dktr,dtc->krc/dot_general | solution.py:99
  449.7 1.0 copy.52
  (60 shorter events, 3.7 us)
Async XLA Ops:
  7.2 52.2 %all-gather.11.cloned.1.call-start = ((), (), s32[]{:S(2)}) async-start(), calls=%async_computation.5 | async-start | bytes 7864320 | tf_op jit(solution)/shard_map/all_gather | solution.py:71
  11.4 118.6 %all-gather.9.cloned.1.call-start = ((), (), s32[]{:S(2)}) async-start(), calls=%async_computation.4 | async-start | bytes 7864320 | tf_op jit(solution)/shard_map/all_gather | solution.py:71
  12.1 163.6 %reduce-scatter.5.cloned.1.call-start = ((), (), s32[]{:S(2)}) async-start(), calls=%async_computation.3 | async-start | bytes 2621440 | tf_op jit(solution)/shard_map/reduce_scatter | solution.py:78
  59.4 11.7 %copy-start.1 = (s32[512]{0:T(512)S(1)}, s32[512]{0:T(512)}, u32[]{:S(2)}) copy-start(s32[512]{0:T(512)} %param.9) | copy-start | bytes 6148
  59.4 11.7 %copy-start = (bf16[512,1024]{1,0:T(8,128)(2,1)S(1)}, bf16[512,1024]{1,0:T(8,128)(2,1)}, u32[]{:S(2)}) copy-start(bf16[512,1024]{1,0:T(8,128)(2,1)} %param.8) | copy-start | bytes 3145732
  59.4 14.2 %copy-start.4 = (f32[1024]{0:T(1024)S(1)}, f32[1024]{0:T(1024)}, u32[]{:S(2)}) copy-start(f32[1024]{0:T(1024)} %param.7) | copy-start | bytes 12292
  71.1 150.1 %reduce-scatter.3.cloned.1.call-start = ((), (), s32[]{:S(2)}) async-start(), calls=%async_computation.2 | async-start | bytes 2621440 | tf_op jit(solution)/shard_map/reduce_scatter | solution.py:78
  71.3 50.6 %collective-permute-start = (bf16[512,1024]{1,0:T(8,128)(2,1)S(1)}, bf16[512,1024]{1,0:T(8,128)(2,1)S(1)}, u32[]{:S(2)}, u32[]{:S(2)}) collective-permute-start(bf16[512,1024]{1,0:T(8,128)(2,1)S(1)} %broadcast_multiply_fusion), channel_id=1, source_target_pairs={{0,0},{1,4},{2,8},{3,12},{4,1},{5,5},{6,9},{7,13},{8,2},{9,6},{10,... | collective-permute-start | bytes 3145736 | tf_op jit(solution)/shard_map/ppermute | solution.py:64
  73.6 48.3 %collective-permute-start.1 = (f32[1024]{0:T(1024)S(1)}, f32[1024]{0:T(1024)S(1)}, u32[]{:S(2)}, u32[]{:S(2)}) collective-permute-start(f32[1024]{0:T(1024)S(1)} %copy-done.4), channel_id=1, source_target_pairs={{0,0},{1,4},{2,8},{3,12},{4,1},{5,5},{6,9},{7,13},{8,2},{9,6},{10,... | collective-permute-start | bytes 12296 | tf_op jit(solution)/shard_map/ppermute | solution.py:64
  141.6 135.2 %all-gather.15.cloned.1.call-start = ((), (), s32[]{:S(2)}) async-start(), calls=%async_computation.7 | async-start | bytes 2621440 | tf_op jit(solution)/shard_map/all_gather | solution.py:105
  231.8 91.7 %all-gather.13.cloned.1.call-start = ((), (), s32[]{:S(2)}) async-start(), calls=%async_computation.6 | async-start | bytes 2621440 | tf_op jit(solution)/shard_map/all_gather | solution.py:105
  276.8 111.2 %collective-permute-start.3 = (bf16[4,512,512]{2,1,0:T(8,128)(2,1)}, bf16[4,512,512]{2,1,0:T(8,128)(2,1)}, u32[]{:S(2)}, u32[]{:S(2)}) collective-permute-start(bf16[4,512,512]{2,1,0:T(8,128)(2,1)} %bitcast.139), channel_id=1, source_target_pairs={{0,1},{1,0},{2,3},{3,2},{4,5},{5,4},{6,7},{7,6},{8,9},{9,8},{10,11... | collective-permute-start | bytes 6291464 | tf_op jit(solution)/shard_map/ppermute | solution.py:111
  277.4 98.1 %collective-permute-start.5 = (bf16[4,512,512]{2,1,0:T(8,128)(2,1)}, bf16[4,512,512]{2,1,0:T(8,128)(2,1)}, u32[]{:S(2)}, u32[]{:S(2)}) collective-permute-start(bf16[4,512,512]{2,1,0:T(8,128)(2,1)} %bitcast.140), channel_id=1, source_target_pairs={{0,2},{1,3},{2,0},{3,1},{4,6},{5,7},{6,4},{7,5},{8,10},{9,11},{10,... | collective-permute-start | bytes 6291464 | tf_op jit(solution)/shard_map/ppermute | solution.py:109
  323.4 76.5 %collective-permute-start.4 = (bf16[4,512,512]{2,1,0:T(8,128)(2,1)}, bf16[4,512,512]{2,1,0:T(8,128)(2,1)}, u32[]{:S(2)}, u32[]{:S(2)}) collective-permute-start(bf16[4,512,512]{2,1,0:T(8,128)(2,1)} %bitcast.136), channel_id=1, source_target_pairs={{0,1},{1,0},{2,3},{3,2},{4,5},{5,4},{6,7},{7,6},{8,9},{9,8},{10,11... | collective-permute-start | bytes 6291464 | tf_op jit(solution)/shard_map/ppermute | solution.py:111
  324.1 97.5 %collective-permute-start.6 = (bf16[4,512,512]{2,1,0:T(8,128)(2,1)}, bf16[4,512,512]{2,1,0:T(8,128)(2,1)}, u32[]{:S(2)}, u32[]{:S(2)}) collective-permute-start(bf16[4,512,512]{2,1,0:T(8,128)(2,1)} %bitcast.137), channel_id=1, source_target_pairs={{0,2},{1,3},{2,0},{3,1},{4,6},{5,7},{6,4},{7,5},{8,10},{9,11},{10,... | collective-permute-start | bytes 6291464 | tf_op jit(solution)/shard_map/ppermute | solution.py:109
  325.3 50.3 %collective-permute-start.2 = (bf16[512,1024]{1,0:T(8,128)(2,1)S(1)}, bf16[512,1024]{1,0:T(8,128)(2,1)S(1)}, u32[]{:S(2)}, u32[]{:S(2)}) collective-permute-start(bf16[512,1024]{1,0:T(8,128)(2,1)S(1)} %get-tuple-element.13), channel_id=1, source_target_pairs={{0,0},{1,4},{2,8},{3,12},{4,1},{5,5},{6,9},{7,13},{8,2},{9,6},{10,... | collective-permute-start | bytes 3145736 | tf_op jit(solution)/shard_map/ppermute | solution.py:64
  327.6 11.3 %copy-start.3 = (bf16[2048,512]{1,0:T(8,128)(2,1)S(1)}, bf16[2048,512]{1,0:T(8,128)(2,1)}, u32[]{:S(2)}) copy-start(bf16[2048,512]{1,0:T(8,128)(2,1)} %all-gather.15.cloned.1.call-done) | copy-start | bytes 6291460
  327.6 22.5 %slice-start = ((s8[6291456]{0:T(1024)(128)(4,1)}), s8[4194304]{0:T(1024)(128)(4,1)S(1)}, s32[]{:S(2)}) async-start(s8[6291456]{0:T(1024)(128)(4,1)} %bitcast.114), calls=%async_computation.8 | async-start | bytes 8388608
  327.6 22.5 %slice-start.4 = ((s8[6291456]{0:T(1024)(128)(4,1)}), s8[4194304]{0:T(1024)(128)(4,1)S(1)}, s32[]{:S(2)}) async-start(s8[6291456]{0:T(1024)(128)(4,1)} %bitcast.127), calls=%async_computation.12 | async-start | bytes 8388608
  338.9 11.2 %slice-start.1 = ((s8[6291456]{0:T(1024)(128)(4,1)}), s8[2097152]{0:T(1024)(128)(4,1)S(1)}, s32[]{:S(2)}) async-start(s8[6291456]{0:T(1024)(128)(4,1)} %bitcast.114), calls=%async_computation.9 | async-start | bytes 4194304
  338.9 11.2 %slice-start.5 = ((s8[6291456]{0:T(1024)(128)(4,1)}), s8[2097152]{0:T(1024)(128)(4,1)S(1)}, s32[]{:S(2)}) async-start(s8[6291456]{0:T(1024)(128)(4,1)} %bitcast.127), calls=%async_computation.13 | async-start | bytes 4194304
  338.9 11.2 %copy-start.2 = (bf16[2048,512]{1,0:T(8,128)(2,1)S(1)}, bf16[2048,512]{1,0:T(8,128)(2,1)}, u32[]{:S(2)}) copy-start(bf16[2048,512]{1,0:T(8,128)(2,1)} %all-gather.13.cloned.1.call-done) | copy-start | bytes 6291460
  375.6 55.8 %collective-permute-start.7 = (bf16[4,512,512]{2,1,0:T(8,128)(2,1)}, bf16[4,512,512]{2,1,0:T(8,128)(2,1)}, u32[]{:S(2)}, u32[]{:S(2)}) collective-permute-start(bf16[4,512,512]{2,1,0:T(8,128)(2,1)} %collective-permute-done.5), channel_id=1, source_target_pairs={{0,1},{1,0},{2,3},{3,2},{4,5},{5,4},{6,7},{7,6},{8,9},{9,8},{10,11... | collective-permute-start | bytes 6291464 | tf_op jit(solution)/shard_map/ppermute | solution.py:112
  382.4 49.1 %collective-permute-start.9 = (f32[1024]{0:T(1024)S(1)}, f32[1024]{0:T(1024)S(1)}, u32[]{:S(2)}, u32[]{:S(2)}) collective-permute-start(f32[1024]{0:T(1024)S(1)} %psum.15), channel_id=1, source_target_pairs={{0,0},{1,4},{2,8},{3,12},{4,1},{5,5},{6,9},{7,13},{8,2},{9,6},{10,... | collective-permute-start | bytes 12296 | tf_op jit(solution)/shard_map/ppermute | solution.py:64
  388.0 23.8 %slice-start.2 = ((s8[6291456]{0:T(1024)(128)(4,1)}), s8[4194304]{0:T(1024)(128)(4,1)S(1)}, s32[]{:S(2)}) async-start(s8[6291456]{0:T(1024)(128)(4,1)} %bitcast.117), calls=%async_computation.10 | async-start | bytes 8388608
  388.0 23.7 %slice-start.6 = ((s8[6291456]{0:T(1024)(128)(4,1)}), s8[4194304]{0:T(1024)(128)(4,1)S(1)}, s32[]{:S(2)}) async-start(s8[6291456]{0:T(1024)(128)(4,1)} %bitcast.130), calls=%async_computation.14 | async-start | bytes 8388608
  400.0 11.8 %slice-start.3 = ((s8[6291456]{0:T(1024)(128)(4,1)}), s8[2097152]{0:T(1024)(128)(4,1)S(1)}, s32[]{:S(2)}) async-start(s8[6291456]{0:T(1024)(128)(4,1)} %bitcast.117), calls=%async_computation.11 | async-start | bytes 4194304
  400.0 11.8 %slice-start.7 = ((s8[6291456]{0:T(1024)(128)(4,1)}), s8[2097152]{0:T(1024)(128)(4,1)S(1)}, s32[]{:S(2)}) async-start(s8[6291456]{0:T(1024)(128)(4,1)} %bitcast.130), calls=%async_computation.15 | async-start | bytes 4194304
  421.6 19.9 %collective-permute-start.8 = (bf16[4,512,512]{2,1,0:T(8,128)(2,1)}, bf16[4,512,512]{2,1,0:T(8,128)(2,1)S(1)}, u32[]{:S(2)}, u32[]{:S(2)}) collective-permute-start(bf16[4,512,512]{2,1,0:T(8,128)(2,1)} %collective-permute-done.6), channel_id=1, source_target_pairs={{0,1},{1,0},{2,3},{3,2},{4,5},{5,4},{6,7},{7,6},{8,9},{9,8},{10,11... | collective-permute-start | bytes 6291464 | tf_op jit(solution)/shard_map/ppermute | solution.py:112
Sparse Core Ops, SparseCore 0:
  11.5 47.8 all-gather.10
  60.9 68.9 all-gather.8
  132.8 42.8 reduce-scatter.4
  177.9 43.1 reduce-scatter.2
  231.9 44.8 all-gather.14
  278.8 44.6 all-gather.12

commit v3 on v2

--- a/solution.py
+++ b/solution.py
@@ -105,9 +105,9 @@
         lax.all_gather(joined_grad[:, c * width : (c + 1) * width], "weight", axis=0)
         for c in range(COLUMN_PARTS)
     ]
-    mine[-1], normed = lax.optimization_barrier((mine[-1], normed))
+    mine[-1], gain_term = lax.optimization_barrier((mine[-1], gain_term))
     far = [lax.ppermute(block, "dp", partner(count, 2)) for block in mine]
-    far[0], gain_term = lax.optimization_barrier((far[0], gain_term))
+    far[0], normed = lax.optimization_barrier((far[0], normed))
     near = [lax.ppermute(block, "dp", partner(count, 1)) for block in mine]
     last = [lax.ppermute(block, "dp", partner(count, 1)) for block in far]
     hidden = turn(normed)

time: 460 us -> 443 us (0.963)
  waiting for transfers between devices: 286 us -> 275 us
  matrix products: 104 us -> 96.5 us
    ppermute x4, waiting for transfers between devices: 61.1 us -> 51.3 us  [turn(): return lax.ppermute(block, ('weight', 'dp'), swap)]
    dot_general x8, matrix products: 81.2 us -> 73.4 us  [put(): jnp.einsum('dktr,dtc->krc', all_tapped, errors, preferred_element_type=jn...]
  transfers between devices with their start and end apart: 16 -> 16, of which waited for: 8 -> 8; matrix products, arithmetic and copies ran while one was open for 24% -> 23% of each run, Pallas kernels for 0% -> 0%
where the time goes in v3:
time: 443 us; the launch traced here: 442 us
  waiting for transfers between devices  275 us (62%)
  matrix products  96.5 us (22%)
  starting transfers between devices  21.3 us (5%)
  local copies, waits for them, and re-layouts  18.2 us (4%)
  between operations  14.3 us (3%)
  blocking collectives  12.5 us (3%)
    all_gather x2, waiting for transfers between devices, on_square(): lax.all_gather(joined_grad[:, c * width:(c + 1) * width], 'weight', axis=0)  89.2 us
    reduce_scatter x2, waiting for transfers between devices, on_square(): lax.psum_scatter(partial, 'weight', scatter_dimension=0, tiled=False)  79.6 us
    dot_general x8, matrix products, put(): jnp.einsum('dktr,dtc->krc', all_tapped, errors, preferred_element_type=jn...  73.4 us
    all_gather x2, waiting for transfers between devices, on_square(): block = lax.all_gather(tapped[:, s * part:(s + 1) * part], 'dp', axis=0)  53.6 us
    ppermute x4, waiting for transfers between devices, turn(): return lax.ppermute(block, ('weight', 'dp'), swap)  51.3 us
    dot_general x2, matrix products, on_square(): jnp.einsum('dktr,krc->dtc', block, join_weight, preferred_element_type=jn...  23.1 us
    ppermute x4, starting transfers between devices, turn(): return lax.ppermute(block, ('weight', 'dp'), swap)  14.5 us
    broadcast_in_dim x1, local copies, waits for them, and re-layouts, on_square(): grad_weight = jnp.zeros((levels, rows, feature_count), jnp.bfloat16)  11.3 us
  transfers between devices with their start and end apart: 16, of which 8 were waited for; matrix products, arithmetic and copies ran while one was open for 23% of the time, Pallas kernels for 0%

profile of v3, /device:TPU:17, one launch (start us, length us, event | category | flops | bytes accessed | tf_op | source)
XLA Modules:
  0.0 441.9 jit_solution(13534134597587110180)
XLA Ops:
  7.2 4.2 fusion.34
  12.5 3.6 collective-permute-start
  16.1 2.9 collective-permute-start.1
  19.0 44.1 %collective-permute-done.1 = f32[1024]{0:T(1024)S(1)} collective-permute-done((f32[1024]{0:T(1024)S(1)}, f32[1024]{0:T(1024)S(1)}, u32[]{:S(2)}, u32[]{:S(2)}) %collective-permute-start.1) | collective-permute-done | bytes 4128 | tf_op jit(solution)/shard_map/ppermute | solution.py:64
  63.0 16.0 %all-gather.9.cloned.1.call-done = bf16[12,256,1024]{2,1,0:T(8,128)(2,1)} async-done(((bf16[3,256,1024]{2,1,0:T(8,128)(2,1)}), bf16[12,256,1024]{2,1,0:T(8,128)(2,1)}) %all-gather.9.cloned.1.call-update) | async-done | bytes 6291472 | tf_op jit(solution)/shard_map/all_gather | solution.py:71
  79.0 11.6 %bitcast_convert_fusion.9 = bf16[4,256,1024]{2,1,0:T(8,128)(2,1)} fusion(bf16[4,3,256,1024]{3,2,1,0:T(8,128)(2,1)} %bitcast.110, bf16[3,1024,1024]{2,1,0:T(8,128)(2,1)} %param.6), kind=kOutput, calls=%fused_computation.14 | convolution fusion | flops 6443499520 | bytes 14680064 | tf_op jit(solution)/shard_map/dktr,krc->dtc/dot_general | solution.py:75
  90.7 37.6 %all-gather.11.cloned.1.call-done = bf16[12,256,1024]{2,1,0:T(8,128)(2,1)} async-done(((bf16[3,256,1024]{2,1,0:T(8,128)(2,1)}), bf16[12,256,1024]{2,1,0:T(8,128)(2,1)}) %all-gather.11.cloned.1.call-update) | async-done | bytes 6291472 | tf_op jit(solution)/shard_map/all_gather | solution.py:71
  128.3 11.5 %bitcast_convert_fusion.8 = bf16[4,256,1024]{2,1,0:T(8,128)(2,1)} fusion(bf16[4,3,256,1024]{3,2,1,0:T(8,128)(2,1)} %bitcast.121, bf16[3,1024,1024]{2,1,0:T(8,128)(2,1)} %param.6), kind=kOutput, calls=%fused_computation.13 | convolution fusion | flops 6443499520 | bytes 14680064 | tf_op jit(solution)/shard_map/dktr,krc->dtc/dot_general | solution.py:75
  139.9 33.6 %reduce-scatter.3.cloned.1.call-done = bf16[1,256,1024]{2,1,0:T(8,128)(2,1)} async-done(((bf16[4,256,1024]{2,1,0:T(8,128)(2,1)}), bf16[1,256,1024]{2,1,0:T(8,128)(2,1)}) %reduce-scatter.3.cloned.1.call-update) | async-done | bytes 524304 | tf_op jit(solution)/shard_map/reduce_scatter | solution.py:78
  173.5 46.0 %reduce-scatter.5.cloned.1.call-done = bf16[1,256,1024]{2,1,0:T(8,128)(2,1)} async-done(((bf16[4,256,1024]{2,1,0:T(8,128)(2,1)}), bf16[1,256,1024]{2,1,0:T(8,128)(2,1)}) %reduce-scatter.5.cloned.1.call-update) | async-done | bytes 524304 | tf_op jit(solution)/shard_map/reduce_scatter | solution.py:78
  219.5 1.8 fusion.19
  221.3 5.6 %psum.14 = f32[2,512]{1,0:T(2,128)S(1)} all-reduce(f32[2,512]{1,0:T(2,128)S(1)} %pad_maximum_fusion.2), channel_id=1, replica_groups=mesh['group'=2,'weight'=4,'dp'=4] {'dp'}, use_global_device_ids=true, to_apply=%region_4.0 | all-reduce | flops 1024 | bytes 8192 | tf_op jit(solution)/shard_map/psum | solution.py:83
  227.0 2.1 fusion.24
  230.8 44.4 %all-gather.13.cloned.1.call-done = bf16[2048,512]{1,0:T(8,128)(2,1)} async-done(((bf16[512,512]{1,0:T(8,128)(2,1)}), bf16[2048,512]{1,0:T(8,128)(2,1)}) %all-gather.13.cloned.1.call-update) | async-done | bytes 2097168 | tf_op jit(solution)/shard_map/all_gather | solution.py:105
  275.8 1.2 collective-permute-start.2
  277.0 44.8 %all-gather.15.cloned.1.call-done = bf16[2048,512]{1,0:T(8,128)(2,1)} async-done(((bf16[512,512]{1,0:T(8,128)(2,1)}), bf16[2048,512]{1,0:T(8,128)(2,1)}) %all-gather.15.cloned.1.call-update) | async-done | bytes 2097168 | tf_op jit(solution)/shard_map/all_gather | solution.py:105
  322.5 1.2 collective-permute-start.6
  323.7 6.8 %psum.15 = f32[1024]{0:T(1024)S(1)} all-reduce(bf16[1024]{0:T(1024)(128)(2,1)S(1)} %get-tuple-element.16), channel_id=1, replica_groups=mesh['group'=2,'weight'=4,'dp'=4] {'weight'}, use_global_device_ids=true, to_apply=%region_6.0 | all-reduce | flops 1024 | bytes 6144 | tf_op jit(solution)/shard_map/psum | solution.py:114
  330.5 5.9 %collective-permute-start.9 = (f32[1024]{0:T(1024)S(1)}, f32[1024]{0:T(1024)S(1)}, u32[]{:S(2)}, u32[]{:S(2)}) collective-permute-start(f32[1024]{0:T(1024)S(1)} %psum.15), channel_id=1, source_target_pairs={{0,0},{1,4},{2,8},{3,12},{4,1},{5,5},{6,9},{7,13},{8,2},{9,6},{10,... | collective-permute-start | bytes 12296 | tf_op jit(solution)/shard_map/ppermute | solution.py:64
  336.4 11.3 %broadcast_in_dim.10 = bf16[3,1024,4096]{2,1,0:T(8,128)(2,1)} broadcast(bf16[]{:T(256)} %constant.10.clone.1), dimensions={} | broadcast | bytes 25165826 | tf_op jit(solution)/shard_map/broadcast_in_dim | solution.py:96
  347.7 11.1 %fusion.4 = bf16[3,1024,4096]{2,1,0:T(8,128)(2,1)} fusion(bf16[3,1024,4096]{2,1,0:T(8,128)(2,1)} %broadcast_in_dim.10, s32[]{:T(128)S(6)} %select_n.24, bf16[4,512,512,1]{2,1,3,0:T(8,128)(2,1)S(1)} %bitcast.137, bf16[4,3,256,1024]{3,2,1,0:T(8,128)(2,1)} %bitcast.122, bf16[4,3,256,1024]{3,2,1,0:T(8,128)(2,1)} %bitcast.111), kind=kOutput, calls=%fused_computation.20 | convolution fusion | flops 6469189632 | bytes 17825796 | tf_op jit(solution)/shard_map/dktr,dtc->krc/dot_general | solution.py:99
  358.9 8.2 %fusion.5 = bf16[3,1024,4096]{2,1,0:T(8,128)(2,1)} fusion(bf16[3,1024,4096]{2,1,0:T(8,128)(2,1)} %fusion.4, s32[]{:T(128)S(6)} %select_n.25, bf16[4,512,512]{2,1,0:T(8,128)(2,1)S(1)} %bitcast.134, bf16[4,3,256,1024]{3,2,1,0:T(8,128)(2,1)S(1)} %bitcast.125, bf16[4,3,256,1024]{3,2,1,0:T(8,128)(2,1)S(1)} %bitcast.114), kind=kOutput, calls=%fused_computation.21 | convolution fusion | flops 6469189632 | bytes 17825796 | tf_op jit(solution)/shard_map/dktr,dtc->krc/dot_general | solution.py:99
  367.2 1.1 collective-permute-start.7
  368.2 2.1 collective-permute-start.3
  370.4 9.8 %fusion.6 = bf16[3,1024,4096]{2,1,0:T(8,128)(2,1)} fusion(bf16[3,1024,4096]{2,1,0:T(8,128)(2,1)} %fusion.5, s32[]{:T(128)S(6)} %select_n.26, bf16[4,512,512]{2,1,0:T(8,128)(2,1)} %collective-permute-done.4, bf16[4,3,256,1024]{3,2,1,0:T(8,128)(2,1)S(1)} %bitcast.126, bf16[4,3,256,1024]{3,2,1,0:T(8,128)(2,1)S(1)} %bitcast.115), kind=kOutput, calls=%fused_computation.22 | convolution fusion | flops 6469189632 | bytes 17825796 | tf_op jit(solution)/shard_map/dktr,dtc->krc/dot_general | solution.py:99
  380.2 9.8 %fusion.7 = bf16[3,1024,4096]{2,1,0:T(8,128)(2,1)} fusion(bf16[3,1024,4096]{2,1,0:T(8,128)(2,1)} %fusion.6, s32[]{:T(128)S(6)} %select_n.27, bf16[4,512,512]{2,1,0:T(8,128)(2,1)} %collective-permute-done.5, bf16[4,3,256,1024]{3,2,1,0:T(8,128)(2,1)S(1)} %bitcast.127, bf16[4,3,256,1024]{3,2,1,0:T(8,128)(2,1)S(1)} %bitcast.116), kind=kOutput, calls=%fused_computation.23 | convolution fusion | flops 6469189632 | bytes 17825796 | tf_op jit(solution)/shard_map/dktr,dtc->krc/dot_general | solution.py:99
  390.0 8.2 %fusion.8 = bf16[3,1024,4096]{2,1,0:T(8,128)(2,1)} fusion(bf16[3,1024,4096]{2,1,0:T(8,128)(2,1)} %fusion.7, s32[]{:T(128)S(6)} %select_n.28, bf16[4,512,512]{2,1,0:T(8,128)(2,1)S(1)} %collective-permute-done.2, bf16[4,3,256,1024]{3,2,1,0:T(8,128)(2,1)S(1)} %bitcast.128, bf16[4,3,256,1024]{3,2,1,0:T(8,128)(2,1)S(1)} %bitcast.117), kind=kOutput, calls=%fused_computation.24 | convolution fusion | flops 6469189632 | bytes 17825796 | tf_op jit(solution)/shard_map/dktr,dtc->krc/dot_general | solution.py:99
  398.2 1.8 collective-permute-start.8
  400.0 9.8 %fusion.9 = bf16[3,1024,4096]{2,1,0:T(8,128)(2,1)} fusion(bf16[3,1024,4096]{2,1,0:T(8,128)(2,1)} %fusion.8, s32[]{:T(128)S(6)} %select_n.29, bf16[4,512,512]{2,1,0:T(8,128)(2,1)} %collective-permute-done.6, bf16[4,3,256,1024]{3,2,1,0:T(8,128)(2,1)S(1)} %bitcast.129, bf16[4,3,256,1024]{3,2,1,0:T(8,128)(2,1)S(1)} %bitcast.118), kind=kOutput, calls=%fused_computation.25 | convolution fusion | flops 6469189632 | bytes 17825796 | tf_op jit(solution)/shard_map/dktr,dtc->krc/dot_general | solution.py:99
  409.8 7.2 %collective-permute-done.3 = bf16[512,1024]{1,0:T(8,128)(2,1)S(1)} collective-permute-done((bf16[512,1024]{1,0:T(8,128)(2,1)S(1)}, bf16[512,1024]{1,0:T(8,128)(2,1)S(1)}, u32[]{:S(2)}, u32[]{:S(2)}) %collective-permute-start.3) | collective-permute-done | bytes 1048608 | tf_op jit(solution)/shard_map/ppermute | solution.py:64
  417.1 8.2 %fusion.10 = bf16[3,1024,4096]{2,1,0:T(8,128)(2,1)} fusion(bf16[3,1024,4096]{2,1,0:T(8,128)(2,1)} %fusion.9, s32[]{:T(128)S(6)} %select_n.30, bf16[4,512,512]{2,1,0:T(8,128)(2,1)S(1)} %collective-permute-done.7, bf16[4,3,256,1024]{3,2,1,0:T(8,128)(2,1)S(1)} %bitcast.130, bf16[4,3,256,1024]{3,2,1,0:T(8,128)(2,1)S(1)} %bitcast.119), kind=kOutput, calls=%fused_computation.26 | convolution fusion | flops 6469189632 | bytes 17825796 | tf_op jit(solution)/shard_map/dktr,dtc->krc/dot_general | solution.py:99
  425.3 8.2 %fusion.11 = bf16[3,1024,4096]{2,1,0:T(8,128)(2,1)} fusion(bf16[3,1024,4096]{2,1,0:T(8,128)(2,1)} %fusion.10, s32[]{:T(128)S(6)} %select_n.31, bf16[4,512,512]{2,1,0:T(8,128)(2,1)S(1)} %collective-permute-done.8, bf16[4,3,256,1024]{3,2,1,0:T(8,128)(2,1)S(1)} %bitcast.131, bf16[4,3,256,1024]{3,2,1,0:T(8,128)(2,1)S(1)} %bitcast.120), kind=kOutput, calls=%fused_computation.27 | convolution fusion | flops 6469189632 | bytes 17825796 | tf_op jit(solution)/shard_map/dktr,dtc->krc/dot_general | solution.py:99
  (50 shorter events, 5.7 us)
Async XLA Ops:
  7.2 5.1 %copy-start.1 = (s32[512]{0:T(512)S(1)}, s32[512]{0:T(512)}, u32[]{:S(2)}) copy-start(s32[512]{0:T(512)} %param.9) | copy-start | bytes 6148
  7.2 5.1 %copy-start = (bf16[512,1024]{1,0:T(8,128)(2,1)S(1)}, bf16[512,1024]{1,0:T(8,128)(2,1)}, u32[]{:S(2)}) copy-start(bf16[512,1024]{1,0:T(8,128)(2,1)} %param.8) | copy-start | bytes 3145732
  7.2 8.9 %copy-start.4 = (f32[1024]{0:T(1024)S(1)}, f32[1024]{0:T(1024)}, u32[]{:S(2)}) copy-start(f32[1024]{0:T(1024)} %param.7) | copy-start | bytes 12292
  7.2 71.8 %all-gather.9.cloned.1.call-start = ((), (), s32[]{:S(2)}) async-start(), calls=%async_computation.4 | async-start | bytes 7864320 | tf_op jit(solution)/shard_map/all_gather | solution.py:71
  11.5 116.8 %all-gather.11.cloned.1.call-start = ((), (), s32[]{:S(2)}) async-start(), calls=%async_computation.5 | async-start | bytes 7864320 | tf_op jit(solution)/shard_map/all_gather | solution.py:71
  12.2 161.2 %reduce-scatter.3.cloned.1.call-start = ((), (), s32[]{:S(2)}) async-start(), calls=%async_computation.2 | async-start | bytes 2621440 | tf_op jit(solution)/shard_map/reduce_scatter | solution.py:78
  12.5 50.6 %collective-permute-start = (bf16[512,1024]{1,0:T(8,128)(2,1)S(1)}, bf16[512,1024]{1,0:T(8,128)(2,1)S(1)}, u32[]{:S(2)}, u32[]{:S(2)}) collective-permute-start(bf16[512,1024]{1,0:T(8,128)(2,1)S(1)} %broadcast_multiply_fusion), channel_id=1, source_target_pairs={{0,0},{1,4},{2,8},{3,12},{4,1},{5,5},{6,9},{7,13},{8,2},{9,6},{10,... | collective-permute-start | bytes 3145736 | tf_op jit(solution)/shard_map/ppermute | solution.py:64
  16.1 47.0 %collective-permute-start.1 = (f32[1024]{0:T(1024)S(1)}, f32[1024]{0:T(1024)S(1)}, u32[]{:S(2)}, u32[]{:S(2)}) collective-permute-start(f32[1024]{0:T(1024)S(1)} %copy-done.4), channel_id=1, source_target_pairs={{0,0},{1,4},{2,8},{3,12},{4,1},{5,5},{6,9},{7,13},{8,2},{9,6},{10,... | collective-permute-start | bytes 12296 | tf_op jit(solution)/shard_map/ppermute | solution.py:64
  90.6 128.9 %reduce-scatter.5.cloned.1.call-start = ((), (), s32[]{:S(2)}) async-start(), calls=%async_computation.3 | async-start | bytes 2621440 | tf_op jit(solution)/shard_map/reduce_scatter | solution.py:78
  139.8 135.3 %all-gather.13.cloned.1.call-start = ((), (), s32[]{:S(2)}) async-start(), calls=%async_computation.6 | async-start | bytes 2621440 | tf_op jit(solution)/shard_map/all_gather | solution.py:105
  230.2 91.7 %all-gather.15.cloned.1.call-start = ((), (), s32[]{:S(2)}) async-start(), calls=%async_computation.7 | async-start | bytes 2621440 | tf_op jit(solution)/shard_map/all_gather | solution.py:105
  275.2 95.2 %collective-permute-start.4 = (bf16[4,512,512]{2,1,0:T(8,128)(2,1)}, bf16[4,512,512]{2,1,0:T(8,128)(2,1)}, u32[]{:S(2)}, u32[]{:S(2)}) collective-permute-start(bf16[4,512,512]{2,1,0:T(8,128)(2,1)} %bitcast.135), channel_id=1, source_target_pairs={{0,1},{1,0},{2,3},{3,2},{4,5},{5,4},{6,7},{7,6},{8,9},{9,8},{10,11... | collective-permute-start | bytes 6291464 | tf_op jit(solution)/shard_map/ppermute | solution.py:111
  275.8 91.3 %collective-permute-start.2 = (bf16[4,512,512]{2,1,0:T(8,128)(2,1)}, bf16[4,512,512]{2,1,0:T(8,128)(2,1)S(1)}, u32[]{:S(2)}, u32[]{:S(2)}) collective-permute-start(bf16[4,512,512]{2,1,0:T(8,128)(2,1)} %bitcast.136), channel_id=1, source_target_pairs={{0,2},{1,3},{2,0},{3,1},{4,6},{5,7},{6,4},{7,5},{8,10},{9,11},{10,... | collective-permute-start | bytes 6291464 | tf_op jit(solution)/shard_map/ppermute | solution.py:109
  321.8 58.4 %collective-permute-start.5 = (bf16[4,512,512]{2,1,0:T(8,128)(2,1)}, bf16[4,512,512]{2,1,0:T(8,128)(2,1)}, u32[]{:S(2)}, u32[]{:S(2)}) collective-permute-start(bf16[4,512,512]{2,1,0:T(8,128)(2,1)} %bitcast.132), channel_id=1, source_target_pairs={{0,1},{1,0},{2,3},{3,2},{4,5},{5,4},{6,7},{7,6},{8,9},{9,8},{10,11... | collective-permute-start | bytes 6291464 | tf_op jit(solution)/shard_map/ppermute | solution.py:111
  322.5 75.7 %collective-permute-start.6 = (bf16[4,512,512]{2,1,0:T(8,128)(2,1)}, bf16[4,512,512]{2,1,0:T(8,128)(2,1)}, u32[]{:S(2)}, u32[]{:S(2)}) collective-permute-start(bf16[4,512,512]{2,1,0:T(8,128)(2,1)} %bitcast.133), channel_id=1, source_target_pairs={{0,2},{1,3},{2,0},{3,1},{4,6},{5,7},{6,4},{7,5},{8,10},{9,11},{10,... | collective-permute-start | bytes 6291464 | tf_op jit(solution)/shard_map/ppermute | solution.py:109
  330.5 36.6 %collective-permute-start.9 = (f32[1024]{0:T(1024)S(1)}, f32[1024]{0:T(1024)S(1)}, u32[]{:S(2)}, u32[]{:S(2)}) collective-permute-start(f32[1024]{0:T(1024)S(1)} %psum.15), channel_id=1, source_target_pairs={{0,0},{1,4},{2,8},{3,12},{4,1},{5,5},{6,9},{7,13},{8,2},{9,6},{10,... | collective-permute-start | bytes 12296 | tf_op jit(solution)/shard_map/ppermute | solution.py:64
  336.4 11.3 %copy-start.3 = (bf16[2048,512]{1,0:T(8,128)(2,1)S(1)}, bf16[2048,512]{1,0:T(8,128)(2,1)}, u32[]{:S(2)}) copy-start(bf16[2048,512]{1,0:T(8,128)(2,1)} %all-gather.13.cloned.1.call-done) | copy-start | bytes 6291460
  336.4 22.5 %slice-start = ((s8[6291456]{0:T(1024)(128)(4,1)}), s8[4194304]{0:T(1024)(128)(4,1)S(1)}, s32[]{:S(2)}) async-start(s8[6291456]{0:T(1024)(128)(4,1)} %bitcast.112), calls=%async_computation.8 | async-start | bytes 8388608
  336.4 22.5 %slice-start.2 = ((s8[6291456]{0:T(1024)(128)(4,1)}), s8[4194304]{0:T(1024)(128)(4,1)S(1)}, s32[]{:S(2)}) async-start(s8[6291456]{0:T(1024)(128)(4,1)} %bitcast.123), calls=%async_computation.10 | async-start | bytes 8388608
  347.7 11.2 %slice-start.1 = ((s8[6291456]{0:T(1024)(128)(4,1)}), s8[2097152]{0:T(1024)(128)(4,1)S(1)}, s32[]{:S(2)}) async-start(s8[6291456]{0:T(1024)(128)(4,1)} %bitcast.112), calls=%async_computation.9 | async-start | bytes 4194304
  347.7 11.2 %slice-start.3 = ((s8[6291456]{0:T(1024)(128)(4,1)}), s8[2097152]{0:T(1024)(128)(4,1)S(1)}, s32[]{:S(2)}) async-start(s8[6291456]{0:T(1024)(128)(4,1)} %bitcast.123), calls=%async_computation.11 | async-start | bytes 4194304
  347.7 11.2 %copy-start.2 = (bf16[2048,512]{1,0:T(8,128)(2,1)S(1)}, bf16[2048,512]{1,0:T(8,128)(2,1)}, u32[]{:S(2)}) copy-start(bf16[2048,512]{1,0:T(8,128)(2,1)} %all-gather.15.cloned.1.call-done) | copy-start | bytes 6291460
  367.2 49.9 %collective-permute-start.7 = (bf16[4,512,512]{2,1,0:T(8,128)(2,1)S(1)}, bf16[4,512,512]{2,1,0:T(8,128)(2,1)S(1)}, u32[]{:S(2)}, u32[]{:S(2)}) collective-permute-start(bf16[4,512,512]{2,1,0:T(8,128)(2,1)S(1)} %collective-permute-done.2), channel_id=1, source_target_pairs={{0,1},{1,0},{2,3},{3,2},{4,5},{5,4},{6,7},{7,6},{8,9},{9,8},{10,11... | collective-permute-start | bytes 6291464 | tf_op jit(solution)/shard_map/ppermute | solution.py:112
  368.2 48.8 %collective-permute-start.3 = (bf16[512,1024]{1,0:T(8,128)(2,1)S(1)}, bf16[512,1024]{1,0:T(8,128)(2,1)S(1)}, u32[]{:S(2)}, u32[]{:S(2)}) collective-permute-start(bf16[512,1024]{1,0:T(8,128)(2,1)S(1)} %get-tuple-element.13), channel_id=1, source_target_pairs={{0,0},{1,4},{2,8},{3,12},{4,1},{5,5},{6,9},{7,13},{8,2},{9,6},{10,... | collective-permute-start | bytes 3145736 | tf_op jit(solution)/shard_map/ppermute | solution.py:64
  398.2 27.1 %collective-permute-start.8 = (bf16[4,512,512]{2,1,0:T(8,128)(2,1)}, bf16[4,512,512]{2,1,0:T(8,128)(2,1)S(1)}, u32[]{:S(2)}, u32[]{:S(2)}) collective-permute-start(bf16[4,512,512]{2,1,0:T(8,128)(2,1)} %collective-permute-done.6), channel_id=1, source_target_pairs={{0,1},{1,0},{2,3},{3,2},{4,5},{5,4},{6,7},{7,6},{8,9},{9,8},{10,11... | collective-permute-start | bytes 6291464 | tf_op jit(solution)/shard_map/ppermute | solution.py:112
Sparse Core Ops, SparseCore 0:
  11.6 67.3 all-gather.8
  81.1 47.0 all-gather.10
  130.6 42.8 reduce-scatter.2
  176.3 43.1 reduce-scatter.4
  230.3 44.8 all-gather.12
  277.1 44.6 all-gather.14
